TPU v7x, 32 devices: a whole 2x2x4 slice. The times are simulated.
32 devices in a mesh: grp: 8 (over z, x), sub: 4 (over y, core).
Axes of the slice: x: 2, y: 2, z: 4, core: 2. Of those that a mesh axis runs over, the one named last changes fastest.
Arguments:
- ocean_state: bfloat16 [8, 131072], P(None, ('grp', 'sub')), may hold values from -6 to 6
- ocean_area: float32 [131072], P(('grp', 'sub')), may hold values from 0.3 to 3
- atm_flux: bfloat16 [12, 32768], P(None, ('grp', 'sub')), may hold values from -6 to 6
- atm_area: float32 [32768], P(('grp', 'sub')), may hold values from 0.3 to 3
- coupling: float32 [12, 8], replicated, may hold values from -2 to 2
- remap_weight: bfloat16 [256, 12, 128, 128], P(('grp', 'sub')), may hold values from -0.21875 to 0.21875
- send_block: int32 [32, 3, 4, 6], P(('grp', 'sub')), may hold values from 0 to 31
- send_count: int32 [32, 3, 4], P(('grp', 'sub')), may hold values from 2 to 6, as said below
- link_slot: int32 [256, 12], P(('grp', 'sub')), may hold values from 0 to 71, as said below
- link_count: int32 [256], P(('grp', 'sub')), may hold values from 1 to 12, as said below
Outputs:
- state_on_atm: bfloat16 [8, 32768], P(None, ('grp', 'sub'))
- flux_on_ocean: bfloat16 [12, 131072], P(None, ('grp', 'sub'))
- imbalance: float32 [12], replicated
Inputs may be any that keep to these rules, and one draw needn't show every extreme that they name: `send_count`: every rank has one route with exactly 6 live slots. `link_slot`: the 12 slots of one atmosphere block differ, and each is a live slot of the sending route. `link_count`: every rank has an atmosphere block with all 12 links live.
All inputs are finite; a program needn't handle non-finite values.
Results may differ from a plain program's by a relative error of at most 0.0075.
Values may be sent and summed in bfloat16 or wider, within the bound.
A program may use at most 64 MiB of HBM per device.

v0:
```python
import math

import jax
import jax.numpy as jnp
from jax import lax
from jax.sharding import PartitionSpec as P


def extended(block, sides, width):
    for axis, dim in sides:
        count = lax.axis_size(axis)
        forward = [(i, i + 1) for i in range(count - 1)]
        forward.append((count - 1, 0))
        backward = [(target, source) for source, target in forward]
        low = lax.ppermute(
            lax.slice_in_dim(block, block.shape[dim] - width, None, axis=dim), axis, forward
        )
        high = lax.ppermute(lax.slice_in_dim(block, 0, width, axis=dim), axis, backward)
        block = jnp.concatenate([low, block, high], axis=dim)
    return block


def state_across(routed):
    wider = extended(routed, (("grp", 0),), 1)
    return wider[0::2]


def state_within(routed):
    return lax.all_to_all(routed, "sub", split_axis=1, concat_axis=1, tiled=True)


def flux_across(partial_value):
    wider = extended(partial_value, (("grp", 0),), 1)
    return wider[0::2]


def flux_within(partial_value):
    return lax.all_to_all(partial_value, "sub", split_axis=1, concat_axis=1, tiled=True)


def shards(
    ocean_state,
    ocean_area,
    atm_flux,
    atm_area,
    coupling,
    remap_weight,
    send_block,
    send_count,
    link_slot,
    link_count,
):
    fields_ocean = ocean_state.shape[0]
    fields_atm = atm_flux.shape[0]
    atm_blocks = remap_weight.shape[0]
    link_total = remap_weight.shape[1]
    width = remap_weight.shape[2]
    ocean_blocks = ocean_state.shape[1] // width
    route_subs = send_block.shape[2]
    capacity = send_block.shape[3]
    slot_total = 3 * route_subs * capacity
    slot_index = lax.broadcasted_iota(jnp.int32, send_block.shape, 3)
    alive_slot = slot_index < send_count[:, :, :, None]
    chosen = jnp.where(alive_slot, send_block, -1).reshape(slot_total)
    chooser = (chosen[:, None] == jnp.arange(ocean_blocks, dtype=jnp.int32)[None, :]).astype(
        jnp.bfloat16
    )
    ocean_blocked = ocean_state.reshape(fields_ocean, ocean_blocks, width)
    routed = jnp.einsum(
        "sb,fbr->sfr", chooser, ocean_blocked, preferred_element_type=jnp.float32
    ).astype(jnp.bfloat16)
    routed = routed.reshape(3, route_subs, capacity, fields_ocean, width)
    arrived = state_within(state_across(routed))
    received = arrived.reshape(slot_total, fields_ocean, width)
    link_flat = link_slot.reshape(-1)
    taken = jnp.take(received, link_flat, axis=0).reshape(
        atm_blocks, link_total, fields_ocean, width
    )
    used_link = lax.broadcasted_iota(jnp.int32, link_slot.shape, 1) < link_count[:, None]
    taken = jnp.where(used_link[:, :, None, None], taken, jnp.zeros((), jnp.bfloat16))
    state_sum = jnp.einsum(
        "alfr,alrq->faq", taken, remap_weight, preferred_element_type=jnp.float32
    )
    flux_blocked = atm_flux.reshape(fields_atm, atm_blocks, width)
    coupled = (
        flux_blocked.astype(jnp.float32)
        + jnp.einsum("gf,faq->gaq", coupling, state_sum, precision=lax.Precision.HIGHEST)
    ).astype(jnp.bfloat16)
    link_part = jnp.einsum(
        "gaq,alrq->algr", coupled, remap_weight, preferred_element_type=jnp.float32
    )
    slot_hits = (
        link_flat[None, :] == jnp.arange(slot_total, dtype=jnp.int32)[:, None]
    ) & used_link.reshape(-1)[None, :]
    slot_hits = slot_hits.astype(jnp.float32)
    slot_part = jnp.dot(
        slot_hits,
        link_part.reshape(atm_blocks * link_total, fields_atm * width),
        precision=lax.Precision.HIGHEST,
    ).astype(jnp.bfloat16)
    slot_part = slot_part.reshape(3, route_subs, capacity, fields_atm, width)
    returned = flux_across(flux_within(slot_part))
    flux_sum = jnp.einsum(
        "sb,sgr->gbr",
        chooser,
        returned.reshape(slot_total, fields_atm, width),
        preferred_element_type=jnp.float32,
    )
    atm_part = jnp.sum(
        atm_area.reshape(atm_blocks, width)[None] * coupled.astype(jnp.float32), axis=(1, 2)
    )
    ocean_part = jnp.sum(ocean_area.reshape(ocean_blocks, width)[None] * flux_sum, axis=(1, 2))
    atm_total, ocean_total = lax.psum((atm_part, ocean_part), ("grp", "sub"))
    devices_all = lax.axis_size("grp") * lax.axis_size("sub")
    norm_scale = 1.0 / math.sqrt(devices_all * atm_blocks * width)
    imbalance = (atm_total - ocean_total) * norm_scale
    state_on_atm = state_sum.reshape(fields_ocean, atm_blocks * width).astype(jnp.bfloat16)
    flux_on_ocean = flux_sum.reshape(fields_atm, ocean_blocks * width).astype(jnp.bfloat16)
    return (state_on_atm, flux_on_ocean, imbalance)


def solution(mesh):
    placed = (
        P(None, ("grp", "sub")),
        P(("grp", "sub")),
        P(None, ("grp", "sub")),
        P(("grp", "sub")),
        P(),
        P(("grp", "sub"), None, None, None),
        P(("grp", "sub"), None, None, None),
        P(("grp", "sub"), None, None),
        P(("grp", "sub"), None),
        P(("grp", "sub")),
    )
    return jax.shard_map(
        shards,
        mesh=mesh,
        in_specs=placed,
        out_specs=(P(None, ("grp", "sub")), P(None, ("grp", "sub")), P()),
        check_vma=False,
    )
```

profile of v0, /device:TPU:0, one launch (start us, length us, event | category | flops | bytes accessed | tf_op | source)
XLA Modules:
  0.0 91.4 jit_solution(5280278191177281849)
XLA Ops:
  0.6 0.0 copy-start
  0.6 0.8 copy.46
  1.5 0.9 fusion.22
  2.4 0.1 eq.28
  2.5 1.1 %convolution_convert_fusion.1 = bf16[72,8,128]{2,0,1:T(8,128)(2,1)S(1)} fusion(bf16[8,32,128]{2,0,1:T(8,128)(2,1)} %bitcast.70, s32[72]{0:T(128)S(1)} %eq.28), kind=kOutput, calls=%fused_computation.2 | convolution fusion | flops 4794624 | bytes 213280 | tf_op jit(solution)/shard_map/sb,fbr->sfr/dot_general | solution.py:69
  3.6 6.0 %collective-permute-start.1 = (bf16[1,4,6,8,128]{4,3,2,1,0:T(8,128)(2,1)S(1)}, bf16[1,4,6,8,128]{4,3,2,1,0:T(8,128)(2,1)}, u32[]{:S(2)}, u32[]{:S(2)}) collective-permute-start(bf16[1,4,6,8,128]{4,3,2,1,0:T(8,128)(2,1)S(1)} %bitcast.71), channel_id=1, source_target_pairs={{4,0},{8,4},{12,8},{16,12},{20,16},{24,20},{28,24},{0,28},{5,1},{9... | collective-permute-start | bytes 147464 | tf_op jit(solution)/shard_map/ppermute | solution.py:18
  9.6 0.0 copy-start.2
  9.6 0.0 copy-start.3
  9.6 0.1 collective-permute-start
  9.7 0.8 reshape.126
  10.5 1.3 %iota_compare_fusion.3 = (pred[8,12]{1,0:T(8,128)(4,1)}, pred[8,12]{1,0:T(8,128)(4,1)}) fusion(s32[8]{0:T(128)} %param.19, s32[8,12]{1,0:T(8,128)} %param.18), kind=kLoop, calls=%fused_computation.37 | loop fusion | flops 672 | bytes 608 | tf_op jit(solution)/shard_map/lt | solution.py:79
  11.8 0.5 fusion.24
  12.3 0.8 reshape.127
  13.1 1.3 %lt.68 = pred[96]{0:T(512)(128)(4,1)} reshape(pred[8,12]{1,0:T(8,128)(4,1)} %get-tuple-element.14) | data formatting | bytes 192 | tf_op jit(solution)/shard_map/lt | solution.py:79
  14.4 0.8 convert_element_type.42
  15.2 0.0 collective-permute-done.1
  15.2 1.4 %collective-permute-done = bf16[1,4,6,8,128]{4,3,2,1,0:T(8,128)(2,1)} collective-permute-done((bf16[1,4,6,8,128]{4,3,2,1,0:T(8,128)(2,1)S(1)}, bf16[1,4,6,8,128]{4,3,2,1,0:T(8,128)(2,1)}, u32[]{:S(2)}, u32[]{:S(2)}) %collective-permute-start) | collective-permute-done | bytes 49184 | tf_op jit(solution)/shard_map/ppermute | solution.py:15
  16.6 0.9 pad_maximum_fusion.1
  17.5 0.7 copy.27
  18.1 3.3 %all-to-all-start = ((bf16[3,4,6,8,128]{4,3,2,0,1:T(8,128)(2,1)}), bf16[3,4,6,8,128]{4,3,2,0,1:T(8,128)(2,1)S(1)}, u32[]{:S(2)}, u32[]{:S(2)}) async-start(bf16[3,4,6,8,128]{4,3,2,0,1:T(8,128)(2,1)} %copy.27), calls=%async_computation | async-start | bytes 294912 | tf_op jit(solution)/shard_map/all_to_all | solution.py:29
  21.5 0.7 pad_clamp_fusion
  22.1 4.1 %all-to-all-done = bf16[3,4,6,8,128]{4,3,2,0,1:T(8,128)(2,1)S(1)} async-done(((bf16[3,4,6,8,128]{4,3,2,0,1:T(8,128)(2,1)}), bf16[3,4,6,8,128]{4,3,2,0,1:T(8,128)(2,1)S(1)}, u32[]{:S(2)}, u32[]{:S(2)}) %all-to-all-start) | async-done | bytes 147488 | tf_op jit(solution)/shard_map/all_to_all | solution.py:29
  26.2 1.3 %gather_fusion = bf16[96,8,128]{2,1,0:T(8,128)(2,1)} fusion(bf16[72,8,128]{2,1,0:T(8,128)(2,1)S(1)} %bitcast.63, s32[1024]{0:T(1024)S(1)} %pad_clamp_fusion), kind=kCustom, calls=%fused_computation | custom fusion | bytes 393600 | tf_op jit(solution)/shard_map/jit(_take)/gather | solution.py:76
  27.6 0.0 copy-done
  27.6 0.0 copy-start.4
  27.6 1.5 %convolution_bitcast_fusion.2 = f32[8,8,128]{2,0,1:T(8,128)S(1)} fusion(bf16[8,12,128,128]{3,2,1,0:T(8,128)(2,1)S(1)} %copy-done, bf16[8,12,8,128]{3,2,1,0:T(8,128)(2,1)} %bitcast.68, pred[8,12]{1,0:T(8,128)(4,1)} %get-tuple-element.15, pred[8,12]{1,0:T(8,128)(4,1)} %get-tuple-element.14), kind=kOutput, calls=%fused_computation.7 | convolution fusion | flops 25362432 | bytes 3375296 | tf_op jit(solution)/shard_map/alfr,alrq->faq/dot_general | solution.py:81
  29.1 0.0 copy-done.2
  29.1 0.0 copy-done.3
  29.1 0.4 multiply_reduce_fusion.1
  29.5 0.9 %fusion.13 = f32[8,12,12,128]{3,1,2,0:T(8,128)S(1)} fusion(bf16[8,12,128,128]{3,2,1,0:T(8,128)(2,1)S(1)} %copy-done, bf16[12,8,128]{2,0,1:T(8,128)(2,1)S(1)} %get-tuple-element.13), kind=kOutput, calls=%fused_computation.23 | convolution fusion | flops 37748736 | bytes 3760128 | tf_op jit(solution)/shard_map/gaq,alrq->algr/dot_general | solution.py:89
  30.4 0.0 copy-start.1
  30.4 0.0 copy-done.4
  30.4 1.3 %convolution_convert_fusion = bf16[72,1536]{1,0:T(8,128)(2,1)} fusion(f32[12,8,12,128]{3,2,1,0:T(8,128)S(1)} %bitcast.62, s32[96]{0:T(128)S(1)} %reshape.127, pred[96]{0:T(512)(128)(4,1)S(1)} %copy-done.4), kind=kOutput, calls=%fused_computation.1 | convolution fusion | flops 127526400 | bytes 811488 | tf_op jit(solution)/shard_map/dot_general | solution.py:96
  31.7 1.1 %reshape.129 = bf16[3,4,6,12,128]{4,3,2,1,0:T(8,128)(2,1)S(1)} reshape(bf16[72,1536]{1,0:T(8,128)(2,1)} %convolution_convert_fusion) | data formatting | bytes 442368 | tf_op jit(solution)/shard_map/reshape | solution.py:101
  32.8 8.8 %all_to_all.10 = bf16[3,4,6,12,128]{4,3,2,0,1:T(8,128)(2,1)S(1)} all-to-all(bf16[3,4,6,12,128]{4,3,2,0,1:T(8,128)(2,1)S(1)} %copy.30), channel_id=1, replica_groups=mesh['grp'=8,'sub'=4] {'sub'}, dimensions={1} | all-to-all | bytes 442368 | tf_op jit(solution)/shard_map/all_to_all | solution.py:38
  41.6 0.1 collective-permute-start.2
  41.6 4.7 %collective-permute-start.3 = (bf16[1,4,6,12,128]{4,3,2,0,1:T(8,128)(2,1)S(1)}, bf16[1,4,6,12,128]{4,3,2,0,1:T(8,128)(2,1)S(1)}, u32[]{:S(2)}, u32[]{:S(2)}) collective-permute-start(bf16[1,4,6,12,128]{4,3,2,0,1:T(8,128)(2,1)S(1)} %get-tuple-element.6), channel_id=1, source_target_pairs={{4,0},{8,4},{12,8},{16,12},{20,16},{24,20},{28,24},{0,28},{5,1},{9... | collective-permute-start | bytes 221192 | tf_op jit(solution)/shard_map/ppermute | solution.py:18
  46.3 0.6 convert_bitcast_fusion
  47.0 2.0 %collective-permute-done.2 = bf16[1,4,6,12,128]{4,3,2,0,1:T(8,128)(2,1)S(1)} collective-permute-done((bf16[1,4,6,12,128]{4,3,2,0,1:T(8,128)(2,1)S(1)}, bf16[1,4,6,12,128]{4,3,2,0,1:T(8,128)(2,1)S(1)}, u32[]{:S(2)}, u32[]{:S(2)}) %collective-permute-start.2) | collective-permute-done | bytes 73760 | tf_op jit(solution)/shard_map/ppermute | solution.py:15
  49.0 0.0 collective-permute-done.3
  49.0 0.1 pad_maximum_fusion
  49.1 0.1 copy.31
  49.2 0.8 reshape.130
  49.9 0.0 copy-done.1
  49.9 1.2 %multiply_reduce_fusion = (f32[12]{0:T(128)S(1)}, bf16[12,32,128]{2,1,0:T(8,128)(2,1)S(1)}) fusion(f32[32,128]{1,0:T(8,128)S(1)} %bitcast.73, bf16[72,12,128]{2,0,1:T(8,128)(2,1)} %reshape.130, s32[72]{0:T(128)S(1)} %eq.28), kind=kOutput, calls=%fused_computation.12 | convolution fusion | flops 7227636 | bytes 336208 | tf_op jit(solution)/shard_map/sb,sgr->gbr/dot_general | solution.py:103
  51.2 0.7 copy.37
  51.9 39.0 %all-reduce = (f32[12]{0:T(128)S(1)}, f32[12]{0:T(128)S(1)}) all-reduce(f32[12]{0:T(128)S(1)} %get-tuple-element.12, f32[12]{0:T(128)S(1)} %get-tuple-element.7), channel_id=1, replica_groups=mesh['grp'=8,'sub'=4] {'grp','sub'}, use_global_device_ids=true, to_apply=%region_1.2 | all-reduce | flops 24 | bytes 192 | tf_op jit(solution)/shard_map/psum | solution.py:113
  90.9 0.5 subtract_multiply_fusion
  (12 shorter events, 0.2 us)
Async XLA Ops:
  0.6 26.9 %copy-start = (bf16[8,12,128,128]{3,2,1,0:T(8,128)(2,1)S(1)}, bf16[8,12,128,128]{3,2,1,0:T(8,128)(2,1)}, u32[]{:S(2)}) copy-start(bf16[8,12,128,128]{3,2,1,0:T(8,128)(2,1)} %param.15) | copy-start | bytes 9437188
  3.6 11.6 %collective-permute-start.1 = (bf16[1,4,6,8,128]{4,3,2,1,0:T(8,128)(2,1)S(1)}, bf16[1,4,6,8,128]{4,3,2,1,0:T(8,128)(2,1)}, u32[]{:S(2)}, u32[]{:S(2)}) collective-permute-start(bf16[1,4,6,8,128]{4,3,2,1,0:T(8,128)(2,1)S(1)} %bitcast.71), channel_id=1, source_target_pairs={{4,0},{8,4},{12,8},{16,12},{20,16},{24,20},{28,24},{0,28},{5,1},{9... | collective-permute-start | bytes 147464 | tf_op jit(solution)/shard_map/ppermute | solution.py:18
  9.6 19.5 %copy-start.2 = (f32[1024]{0:T(1024)S(1)}, f32[1024]{0:T(1024)}, u32[]{:S(2)}) copy-start(f32[1024]{0:T(1024)} %param.13) | copy-start | bytes 12292
  9.6 19.5 %copy-start.3 = (f32[12,8]{0,1:T(8,128)S(1)}, f32[12,8]{0,1:T(8,128)}, u32[]{:S(2)}) copy-start(f32[12,8]{0,1:T(8,128)} %param.14) | copy-start | bytes 1156
  9.6 6.9 %collective-permute-start = (bf16[1,4,6,8,128]{4,3,2,1,0:T(8,128)(2,1)S(1)}, bf16[1,4,6,8,128]{4,3,2,1,0:T(8,128)(2,1)}, u32[]{:S(2)}, u32[]{:S(2)}) collective-permute-start(bf16[1,4,6,8,128]{4,3,2,1,0:T(8,128)(2,1)S(1)} %bitcast.72), channel_id=1, source_target_pairs={{0,4},{4,8},{8,12},{12,16},{16,20},{20,24},{24,28},{28,0},{1,5},{5... | collective-permute-start | bytes 147464 | tf_op jit(solution)/shard_map/ppermute | solution.py:15
  18.1 8.1 %all-to-all-start = ((bf16[3,4,6,8,128]{4,3,2,0,1:T(8,128)(2,1)}), bf16[3,4,6,8,128]{4,3,2,0,1:T(8,128)(2,1)S(1)}, u32[]{:S(2)}, u32[]{:S(2)}) async-start(bf16[3,4,6,8,128]{4,3,2,0,1:T(8,128)(2,1)} %copy.27), calls=%async_computation | async-start | bytes 294912 | tf_op jit(solution)/shard_map/all_to_all | solution.py:29
  27.6 2.8 %copy-start.4 = (pred[96]{0:T(512)(128)(4,1)S(1)}, pred[96]{0:T(512)(128)(4,1)}, u32[]{:S(2)}) copy-start(pred[96]{0:T(512)(128)(4,1)} %lt.68) | copy-start | bytes 292
  30.4 19.5 %copy-start.1 = (f32[4096]{0:T(1024)S(1)}, f32[4096]{0:T(1024)}, u32[]{:S(2)}) copy-start(f32[4096]{0:T(1024)} %param.11) | copy-start | bytes 49156
  41.6 7.4 %collective-permute-start.2 = (bf16[1,4,6,12,128]{4,3,2,0,1:T(8,128)(2,1)S(1)}, bf16[1,4,6,12,128]{4,3,2,0,1:T(8,128)(2,1)S(1)}, u32[]{:S(2)}, u32[]{:S(2)}) collective-permute-start(bf16[1,4,6,12,128]{4,3,2,0,1:T(8,128)(2,1)S(1)} %get-tuple-element.5), channel_id=1, source_target_pairs={{0,4},{4,8},{8,12},{12,16},{16,20},{20,24},{24,28},{28,0},{1,5},{5... | collective-permute-start | bytes 221192 | tf_op jit(solution)/shard_map/ppermute | solution.py:15
  41.6 7.3 %collective-permute-start.3 = (bf16[1,4,6,12,128]{4,3,2,0,1:T(8,128)(2,1)S(1)}, bf16[1,4,6,12,128]{4,3,2,0,1:T(8,128)(2,1)S(1)}, u32[]{:S(2)}, u32[]{:S(2)}) collective-permute-start(bf16[1,4,6,12,128]{4,3,2,0,1:T(8,128)(2,1)S(1)} %get-tuple-element.6), channel_id=1, source_target_pairs={{4,0},{8,4},{12,8},{16,12},{20,16},{24,20},{28,24},{0,28},{5,1},{9... | collective-permute-start | bytes 221192 | tf_op jit(solution)/shard_map/ppermute | solution.py:18
where the time goes:
time: 92.1 us; the launch traced here: 91.4 us
  blocking collectives  47.7 us (52%)
  starting transfers between devices  14.2 us (15%)
  local copies, waits for them, and re-layouts  8.56 us (9%)
  waiting for transfers between devices  7.49 us (8%)
  matrix products  6.39 us (7%)
  other arithmetic  6.23 us (7%)
    psum x1, blocking collectives, shards(): atm_total, ocean_total = lax.psum((atm_part, ocean_part), ('grp', 'sub'))  39 us
    ppermute x2, starting transfers between devices, extended(): lax.ppermute(lax.slice_in_dim(block, 0, width, axis=dim), axis, backward)  10.7 us
    all_to_all x1, blocking collectives, flux_within(): lax.all_to_all(partial_value, 'sub', split_axis=1, concat_axis=1, tiled=T...  8.75 us
    all_to_all x1, waiting for transfers between devices, state_within(): lax.all_to_all(routed, 'sub', split_axis=1, concat_axis=1, tiled=True)  4.11 us
    ppermute x2, waiting for transfers between devices, extended(): lax.ppermute(lax.slice_in_dim(block, block.shape[dim] - width, None, axis...  3.38 us
    all_to_all x1, starting transfers between devices, state_within(): lax.all_to_all(routed, 'sub', split_axis=1, concat_axis=1, tiled=True)  3.33 us
  transfers between devices with their start and end apart: 5, of which 3 were waited for; matrix products, arithmetic and copies ran while one was open for 7% of the time, Pallas kernels for 0%

commit v1 on v0

v1 whole, which is shorter than its diff:
```python
import functools
import math

import jax
import jax.numpy as jnp
from jax import lax
from jax.experimental import pallas as pl
from jax.experimental.pallas import tpu as pltpu
from jax.sharding import PartitionSpec as P

MESH = pl.DeviceIdType.MESH


def kernel(
    groups,
    subs,
    norm_scale,
    state_hbm,
    ocean_area_hbm,
    flux_hbm,
    atm_area_hbm,
    coupling_hbm,
    weight_hbm,
    block_hbm,
    count_hbm,
    link_slot_hbm,
    link_count_hbm,
    state_out,
    flux_out,
    imbalance_out,
    state_in,
    ocean_area_in,
    flux_in,
    atm_area_in,
    coupling_in,
    weight_in,
    block_in,
    count_in,
    link_slot_in,
    link_count_in,
    state_wide,
    state_send,
    state_recv,
    arrived,
    area_send,
    area_recv,
    parts,
    slot_hits,
    chooser,
    flux_send,
    flux_recv,
    sub_parts,
    grp_parts,
    load_sem,
    state_sems,
    area_sems,
    flux_sems,
    sub_sems,
    grp_sems,
):
    f32, bf16, i32 = jnp.float32, jnp.bfloat16, jnp.int32
    ocean_blocks = state_wide.shape[0]
    fields_ocean = state_wide.shape[1]
    width = state_wide.shape[2]
    fields_atm = flux_in.shape[0]
    atm_blocks, link_total = weight_in.shape[:2]
    capacity = block_in.shape[3]
    routes = 3 * subs
    links = atm_blocks * link_total
    quad_rows = 4 * capacity
    flux_rows = flux_send.shape[1]
    me_grp = lax.axis_index("grp")
    me_sub = lax.axis_index("sub")

    pairs = [
        (block_hbm, block_in),
        (count_hbm, count_in),
        (state_hbm, state_in),
        (ocean_area_hbm, ocean_area_in),
        (link_slot_hbm, link_slot_in),
        (link_count_hbm, link_count_in),
        (coupling_hbm, coupling_in),
        (flux_hbm, flux_in),
        (atm_area_hbm, atm_area_in),
        (weight_hbm, weight_in),
    ]
    loads = [
        pltpu.make_async_copy(source, target, load_sem.at[n])
        for n, (source, target) in enumerate(pairs)
    ]
    for load in loads:
        load.start()

    steps = [(o, t) for o in (0, 2) for t in range(subs)] + [(1, t) for t in range(1, subs)]

    def grp_at(offset):
        return lax.rem(me_grp + offset + groups, groups)

    def sub_at(t):
        return lax.rem(me_sub + t, subs)

    barrier = pltpu.get_barrier_semaphore()
    partners = [(grp_at(o - 1), sub_at(t)) for o, t in steps]
    partners += [(grp_at(d), me_sub) for d in range(2, groups - 1)]
    for partner in partners:
        pl.semaphore_signal(barrier, inc=1, device_id=partner, device_id_type=MESH)

    def exchange(source, target, sems, o, t):
        k = sub_at(t)
        return pltpu.make_async_remote_copy(
            src_ref=source.at[o * subs + k],
            dst_ref=target.at[(2 - o) * subs + me_sub],
            send_sem=sems.at[0, o, t],
            recv_sem=sems.at[1, o, t],
            device_id=(grp_at(o - 1), k),
            device_id_type=MESH,
        )

    for n in range(3):
        loads[n].wait()
    for b in range(ocean_blocks):
        state_wide[b] = state_in[:, b * width : (b + 1) * width].astype(f32)

    def alive(o, k, c):
        return jnp.where(c < count_in[0, o, k], 1.0, 0.0).astype(f32)

    def fill_state(o, t):
        k = sub_at(t)
        rows = [
            state_wide[block_in[0, o, k, c]] * alive(o, k, c) for c in range(capacity)
        ]
        return jnp.concatenate(rows, axis=0).astype(bf16)

    state_copies = []
    for n, (o, t) in enumerate(steps):
        state_send[o * subs + sub_at(t)] = fill_state(o, t)
        if n == 0:
            pl.semaphore_wait(barrier, len(partners))
        copy = exchange(state_send, state_recv, state_sems, o, t)
        copy.start()
        state_copies.append(copy)
    state_recv[subs + me_sub] = fill_state(1, 0)

    loads[3].wait()
    area_copies = []
    for o, t in steps + [(1, 0)]:
        k = sub_at(t)
        target = area_recv if (o, t) == (1, 0) else area_send
        for c in range(capacity):
            target[o * subs + k, c : c + 1, :] = ocean_area_in[block_in[0, o, k, c]] * alive(
                o, k, c
            )
        if (o, t) != (1, 0):
            copy = exchange(area_send, area_recv, area_sems, o, t)
            copy.start()
            area_copies.append(copy)

    for n in range(4, 9):
        loads[n].wait()
    lane = lax.broadcasted_iota(i32, (1, 4 * links), 1)
    link_of = lane % links
    quad_of = lane // links
    key = jnp.full((1, 4 * links), -1, i32)
    for a in range(atm_blocks):
        for l in range(link_total):
            slot = link_slot_in[a, l]
            row = (slot // capacity) * quad_rows + slot % capacity
            row = jnp.where(l < link_count_in[a], row, -quad_rows)
            key = jnp.where(link_of == a * link_total + l, row, key)
    key = key + quad_of * capacity
    key = jnp.where(key < 0, -1, key)
    row_of = lax.broadcasted_iota(i32, (routes * quad_rows, 4 * links), 0)
    slot_hits[...] = jnp.where(row_of == key, 1.0, 0.0).astype(bf16)

    lane = lax.broadcasted_iota(i32, (1, routes * flux_rows), 1)
    inner = lane % flux_rows
    slot_of = (lane // flux_rows) * capacity + inner % capacity
    key = jnp.full((1, routes * flux_rows), -1, i32)
    for o in range(3):
        for k in range(subs):
            for c in range(capacity):
                block = jnp.where(c < count_in[0, o, k], block_in[0, o, k, c] * 16, -32)
                key = jnp.where(slot_of == (o * subs + k) * capacity + c, block, key)
    key = key + inner // capacity
    key = jnp.where(inner < fields_atm * capacity, key, -1)
    for part in range(4):
        rows = ocean_blocks * 4
        row_of = lax.broadcasted_iota(i32, (rows, routes * flux_rows), 0) + part * rows
        chooser[part * rows : (part + 1) * rows, :] = jnp.where(row_of == key, 1.0, 0.0).astype(
            bf16
        )
    coefficient = [
        jnp.broadcast_to(coupling_in[:, f : f + 1], (fields_atm, width))
        for f in range(fields_ocean)
    ]

    for copy in state_copies:
        copy.wait_recv()
    loads[9].wait()
    for p in range(routes):
        arrived[p * capacity : (p + 1) * capacity] = (
            state_recv[p].astype(f32).reshape(capacity, fields_ocean, width)
        )

    atm_acc = jnp.zeros((fields_atm, width), f32)
    for a in range(atm_blocks):
        taken = []
        for l in range(link_total):
            used = jnp.where(l < link_count_in[a], 1.0, 0.0).astype(f32)
            taken.append(arrived[link_slot_in[a, l]] * used)
        taken = jnp.concatenate(taken, axis=1).astype(bf16)
        weight = weight_in[a].reshape(link_total * width, width)
        state_sum = jnp.dot(taken, weight, preferred_element_type=f32)
        here = slice(a * width, (a + 1) * width)
        state_out[:, here] = state_sum.astype(bf16)
        value = flux_in[:, here].astype(f32)
        change = coefficient[0] * state_sum[0:1]
        for f in range(1, fields_ocean):
            change = change + coefficient[f] * state_sum[f : f + 1]
        coupled = (value + change).astype(bf16)
        atm_acc = atm_acc + atm_area_in[a : a + 1, :] * coupled.astype(f32)
        part = lax.dot_general(
            coupled, weight, (((1,), (1,)), ((), ())), preferred_element_type=f32
        )
        for l in range(link_total):
            parts[pl.ds(a * link_total + l, fields_atm, stride=links), :] = part[
                :, l * width : (l + 1) * width
            ]

    quads = []
    for q in range(fields_atm // 4):
        operand = parts[q * 4 * links : (q + 1) * 4 * links, :].astype(bf16)
        quads.append(jnp.dot(slot_hits[...], operand, preferred_element_type=f32))
    blank = jnp.zeros((flux_rows - fields_atm * capacity, width), f32)
    for p in range(routes):
        rows = [quad[p * quad_rows : (p + 1) * quad_rows] for quad in quads]
        flux_send[p] = jnp.concatenate(rows + [blank], axis=0).astype(bf16)
    flux_copies = []
    for o, t in steps:
        copy = exchange(flux_send, flux_recv, flux_sems, o, t)
        copy.start()
        flux_copies.append(copy)
    flux_recv[subs + me_sub] = flux_send[subs + me_sub]

    for copy in area_copies:
        copy.wait_recv()
    ocean_acc = [jnp.zeros((quad_rows, width), f32) for _ in quads]
    for p in range(routes):
        area = area_recv[p][:capacity]
        area = jnp.concatenate([area] * 4, axis=0)
        for q, quad in enumerate(quads):
            rounded = quad[p * quad_rows : (p + 1) * quad_rows].astype(bf16).astype(f32)
            ocean_acc[q] = ocean_acc[q] + rounded * area

    def to_lanes(column, group):
        rows = column.shape[0]
        row_of = lax.broadcasted_iota(i32, (rows, 128), 0) // group
        lane_of = lax.broadcasted_iota(i32, (rows, 128), 1)
        return jnp.sum(jnp.where(row_of == lane_of, column, 0.0), axis=0, keepdims=True)

    ocean_rows = jnp.concatenate(ocean_acc, axis=0)
    mine = to_lanes(jnp.sum(atm_acc, axis=1, keepdims=True), 1) - to_lanes(
        jnp.sum(ocean_rows, axis=1, keepdims=True), capacity
    )
    sub_parts[me_sub] = jnp.broadcast_to(mine, (8, 128))
    sub_copies = []
    for t in range(1, subs):
        copy = pltpu.make_async_remote_copy(
            src_ref=sub_parts.at[me_sub],
            dst_ref=sub_parts.at[me_sub],
            send_sem=sub_sems.at[0, t],
            recv_sem=sub_sems.at[1, t],
            device_id=(me_grp, sub_at(t)),
            device_id_type=MESH,
        )
        copy.start()
        sub_copies.append(copy)
    for copy in sub_copies:
        copy.wait_recv()
    total = sub_parts[0]
    for k in range(1, subs):
        total = total + sub_parts[k]
    grp_parts[me_grp] = total
    grp_copies = []
    for d in range(1, groups):
        copy = pltpu.make_async_remote_copy(
            src_ref=grp_parts.at[me_grp],
            dst_ref=grp_parts.at[me_grp],
            send_sem=grp_sems.at[0, d],
            recv_sem=grp_sems.at[1, d],
            device_id=(grp_at(d), me_sub),
            device_id_type=MESH,
        )
        copy.start()
        grp_copies.append(copy)

    for copy in flux_copies:
        copy.wait_recv()
    returned = flux_recv[...].reshape(routes * flux_rows, width)
    flux_sum = jnp.dot(chooser[...], returned, preferred_element_type=f32)
    for b in range(ocean_blocks):
        flux_out[:, b * width : (b + 1) * width] = flux_sum[
            b * 16 : b * 16 + fields_atm
        ].astype(bf16)

    for copy in grp_copies:
        copy.wait_recv()
    total = grp_parts[0]
    for i in range(1, groups):
        total = total + grp_parts[i]
    imbalance_out[...] = total * norm_scale
    for copy in state_copies + area_copies + flux_copies + sub_copies + grp_copies:
        copy.wait_send()


def shards(
    groups,
    subs,
    ocean_state,
    ocean_area,
    atm_flux,
    atm_area,
    coupling,
    remap_weight,
    send_block,
    send_count,
    link_slot,
    link_count,
):
    f32, bf16, i32 = jnp.float32, jnp.bfloat16, jnp.int32
    fields_ocean = ocean_state.shape[0]
    fields_atm = atm_flux.shape[0]
    atm_blocks, link_total, width = remap_weight.shape[:3]
    ocean_blocks = ocean_state.shape[1] // width
    capacity = send_block.shape[3]
    routes = 3 * subs
    links = atm_blocks * link_total
    flux_rows = -(-fields_atm * capacity // 16) * 16
    norm_scale = 1.0 / math.sqrt(groups * subs * atm_blocks * width)
    anywhere = pl.BlockSpec(memory_space=pl.ANY)
    vmem = pl.BlockSpec(memory_space=pltpu.VMEM)
    state_on_atm, flux_on_ocean, imbalance = pl.pallas_call(
        functools.partial(kernel, groups, subs, norm_scale),
        out_shape=(
            jax.ShapeDtypeStruct((fields_ocean, atm_blocks * width), bf16),
            jax.ShapeDtypeStruct((fields_atm, ocean_blocks * width), bf16),
            jax.ShapeDtypeStruct((8, 128), f32),
        ),
        in_specs=[anywhere] * 10,
        out_specs=(vmem, vmem, vmem),
        scratch_shapes=[
            pltpu.VMEM(ocean_state.shape, bf16),
            pltpu.VMEM((ocean_blocks, 1, width), f32),
            pltpu.VMEM(atm_flux.shape, bf16),
            pltpu.VMEM((atm_blocks, width), f32),
            pltpu.VMEM(coupling.shape, f32),
            pltpu.VMEM(remap_weight.shape, bf16),
            pltpu.SMEM(send_block.shape, i32),
            pltpu.SMEM(send_count.shape, i32),
            pltpu.SMEM(link_slot.shape, i32),
            pltpu.SMEM(link_count.shape, i32),
            pltpu.VMEM((ocean_blocks, fields_ocean, width), f32),
            pltpu.VMEM((routes, capacity * fields_ocean, width), bf16),
            pltpu.VMEM((routes, capacity * fields_ocean, width), bf16),
            pltpu.VMEM((routes * capacity, fields_ocean, width), f32),
            pltpu.VMEM((routes, 8, width), f32),
            pltpu.VMEM((routes, 8, width), f32),
            pltpu.VMEM((fields_atm * links, width), f32),
            pltpu.VMEM((routes * 4 * capacity, 4 * links), bf16),
            pltpu.VMEM((ocean_blocks * 16, routes * flux_rows), bf16),
            pltpu.VMEM((routes, flux_rows, width), bf16),
            pltpu.VMEM((routes, flux_rows, width), bf16),
            pltpu.VMEM((subs, 8, 128), f32),
            pltpu.VMEM((groups, 8, 128), f32),
            pltpu.SemaphoreType.DMA((10,)),
            pltpu.SemaphoreType.DMA((2, 3, subs)),
            pltpu.SemaphoreType.DMA((2, 3, subs)),
            pltpu.SemaphoreType.DMA((2, 3, subs)),
            pltpu.SemaphoreType.DMA((2, subs)),
            pltpu.SemaphoreType.DMA((2, groups)),
        ],
        compiler_params=pltpu.CompilerParams(
            collective_id=0, has_side_effects=True, vmem_limit_bytes=40 * 1024 * 1024
        ),
    )(
        ocean_state,
        ocean_area.reshape(ocean_blocks, 1, width),
        atm_flux,
        atm_area.reshape(atm_blocks, width),
        coupling,
        remap_weight,
        send_block,
        send_count,
        link_slot,
        link_count,
    )
    return state_on_atm, flux_on_ocean, imbalance[0, :fields_atm]


def solution(mesh):
    placed = (
        P(None, ("grp", "sub")),
        P(("grp", "sub")),
        P(None, ("grp", "sub")),
        P(("grp", "sub")),
        P(),
        P(("grp", "sub"), None, None, None),
        P(("grp", "sub"), None, None, None),
        P(("grp", "sub"), None, None),
        P(("grp", "sub"), None),
        P(("grp", "sub")),
    )
    return jax.shard_map(
        functools.partial(shards, mesh.shape["grp"], mesh.shape["sub"]),
        mesh=mesh,
        in_specs=placed,
        out_specs=(P(None, ("grp", "sub")), P(None, ("grp", "sub")), P()),
        check_vma=False,
    )
```

time: 92.1 us -> 35.4 us (0.38)
  blocking collectives: 47.7 us -> 0 us
  Pallas kernels: 0 us -> 24.1 us
  starting transfers between devices: 14.2 us -> 0 us
  waiting for transfers between devices: 7.49 us -> 0 us
  matrix products: 6.39 us -> 0 us
  other arithmetic: 6.23 us -> 0 us
  local copies, waits for them, and re-layouts: 8.56 us -> 10.1 us
    psum x1 -> x0, blocking collectives: 39 us -> none  [shards(): atm_total, ocean_total = lax.psum((atm_part, ocean_part), ('grp', 'sub'))]
    pallas_call x0 -> x1, Pallas kernels: none -> 24.1 us  [shards(): pl.pallas_call(functools.partial(kernel, groups, subs, norm_scale), out_s...]
    ppermute x4 -> x0, starting transfers between devices: 10.9 us -> none  [the longest x2 10.7 us: extended(): lax.ppermute(lax.slice_in_dim(block, 0, width, axis=dim), axis, backward)]
    all_to_all x1 -> x0, blocking collectives: 8.75 us -> none  [flux_within(): lax.all_to_all(partial_value, 'sub', split_axis=1, concat_axis=1, tiled=T...]
    unnamed x14 -> x20, local copies, waits for them, and re-layouts: 1.6 us -> 9.63 us
    dot_general x6 -> x0, matrix products: 6.39 us -> none  [the longest x1 1.51 us: shards(): jnp.einsum('alfr,alrq->faq', taken, remap_weight, preferred_element_type=...]
    all_to_all x1 -> x0, waiting for transfers between devices: 4.11 us -> none  [state_within(): lax.all_to_all(routed, 'sub', split_axis=1, concat_axis=1, tiled=True)]
    reshape x5 -> x0, local copies, waits for them, and re-layouts: 3.42 us -> none  [the longest x2 1.53 us: shards(): link_flat = link_slot.reshape(-1)]
  transfers between devices with their start and end apart: 5 -> 0, of which waited for: 3 -> 0; matrix products, arithmetic and copies ran while one was open for 7% -> 0% of each run, Pallas kernels for 0% -> 0%
where the time goes in v1:
time: 35.4 us; the launch traced here: 34.9 us
  Pallas kernels  24.1 us (68%)
  local copies, waits for them, and re-layouts  10.1 us (29%)
  between operations  0.65 us (2%)
    pallas_call x1, Pallas kernels, shards(): pl.pallas_call(functools.partial(kernel, groups, subs, norm_scale), out_s...  24.1 us
    unnamed x20, local copies, waits for them, and re-layouts  9.63 us

profile of v1, /device:TPU:0, one launch (start us, length us, event | category | flops | bytes accessed | tf_op | source)
XLA Modules:
  0.0 34.9 jit_solution(3639504886099876749)
XLA Ops:
  0.6 0.7 %copy.14.count_hbm = s32[1,3,4]{2,1,0:T(4,128)S(1)} copy(s32[1,3,4]{2,0,1:T(1,128)} %param.17) | data formatting | bytes 96 | tf_op args[7]
  1.3 0.8 %copy.13.coupling_hbm = f32[12,8]{1,0:T(8,128)S(1)} copy(f32[12,8]{0,1:T(8,128)} %param.14) | data formatting | bytes 768 | tf_op args[4]
  2.1 0.0 copy-start
  2.1 1.9 %copy-done = bf16[8,12,128,128]{3,2,1,0:T(8,128)(2,1)S(1)} copy-done((bf16[8,12,128,128]{3,2,1,0:T(8,128)(2,1)S(1)}, bf16[8,12,128,128]{3,2,1,0:T(8,128)(2,1)}, u32[]{:S(2)}) %copy-start) | copy-done | bytes 3145752
  4.0 0.0 copy-start.1
  4.0 0.8 %copy-done.1 = bf16[8,4096]{1,0:T(8,128)(2,1)S(1)} copy-done((bf16[8,4096]{1,0:T(8,128)(2,1)S(1)}, bf16[8,4096]{1,0:T(8,128)(2,1)}, u32[]{:S(2)}) %copy-start.1) | copy-done | bytes 65560
  4.8 0.0 copy-start.2
  4.8 0.8 %copy-done.2 = bf16[12,1024]{1,0:T(8,128)(2,1)S(1)} copy-done((bf16[12,1024]{1,0:T(8,128)(2,1)S(1)}, bf16[12,1024]{1,0:T(8,128)(2,1)}, u32[]{:S(2)}) %copy-start.2) | copy-done | bytes 24600
  5.6 0.0 copy-start.3
  5.6 0.7 %copy-done.3 = f32[4096]{0:T(1024)S(1)} copy-done((f32[4096]{0:T(1024)S(1)}, f32[4096]{0:T(1024)}, u32[]{:S(2)}) %copy-start.3) | copy-done | bytes 16408
  6.3 0.0 copy-start.4
  6.3 0.7 %copy-done.4 = s32[1,3,4,6]{3,2,1,0:T(4,128)S(1)} copy-done((s32[1,3,4,6]{3,2,1,0:T(4,128)S(1)}, s32[1,3,4,6]{3,2,1,0:T(4,128)}, u32[]{:S(2)}) %copy-start.4) | copy-done | bytes 312
  7.0 0.0 copy-start.5
  7.0 0.7 %copy-done.5 = f32[1024]{0:T(1024)S(1)} copy-done((f32[1024]{0:T(1024)S(1)}, f32[1024]{0:T(1024)}, u32[]{:S(2)}) %copy-start.5) | copy-done | bytes 4120
  7.7 0.0 copy-start.6
  7.7 0.7 %copy-done.6 = s32[8,12]{1,0:T(8,128)S(1)} copy-done((s32[8,12]{1,0:T(8,128)S(1)}, s32[8,12]{1,0:T(8,128)}, u32[]{:S(2)}) %copy-start.6) | copy-done | bytes 408
  8.4 0.0 copy-start.7
  8.4 0.7 %copy-done.7 = s32[8]{0:T(128)S(1)} copy-done((s32[8]{0:T(128)S(1)}, s32[8]{0:T(128)}, u32[]{:S(2)}) %copy-start.7) | copy-done | bytes 56
  9.0 24.1 %shard_map.121 = (bf16[8,1024]{1,0:T(8,128)(2,1)S(1)}, bf16[12,4096]{1,0:T(8,128)(2,1)S(1)}, f32[8,128]{1,0:T(8,128)S(1)}) custom-call(bf16[8,4096]{1,0:T(8,128)(2,1)S(1)} %copy-done.1, f32[32,1,128]{2,1,0:T(1,128)S(1)} %bitcast.4, bf16[12,1024]{1,0:T(8,128)(2,1)S(1)} %copy-done.2, f32[8,128]{1,0:T(8,128)S(1)} %bitcast.5, f32[12,8]{1,0:T(8,128)S(1)} %copy.13.coupling_hbm, ...), custom_call_target="tpu_custom_call" | custom-call | tf_op jit(solution)/shard_map/pallas_call | solution.py:342
  33.1 0.5 %slice_bitcast_fusion = f32[12]{0:T(128)} fusion(f32[8,128]{1,0:T(8,128)S(1)} %get-tuple-element.8), kind=kLoop, calls=%fused_computation | loop fusion | bytes 96 | tf_op jit(solution)/shard_map/squeeze | solution.py:397
  33.6 0.6 %copy.17 = bf16[8,1024]{1,0:T(8,128)(2,1)} copy(bf16[8,1024]{1,0:T(8,128)(2,1)S(1)} %get-tuple-element.12) | data formatting | bytes 32768
  34.2 0.7 %copy.18 = bf16[12,4096]{1,0:T(8,128)(2,1)} copy(bf16[12,4096]{1,0:T(8,128)(2,1)S(1)} %get-tuple-element.13) | data formatting | bytes 196608
Async XLA Ops:
  2.1 1.9 %copy-start = (bf16[8,12,128,128]{3,2,1,0:T(8,128)(2,1)S(1)}, bf16[8,12,128,128]{3,2,1,0:T(8,128)(2,1)}, u32[]{:S(2)}) copy-start(bf16[8,12,128,128]{3,2,1,0:T(8,128)(2,1)} %weight_hbm.1) | copy-start | bytes 9437188
  4.0 0.8 %copy-start.1 = (bf16[8,4096]{1,0:T(8,128)(2,1)S(1)}, bf16[8,4096]{1,0:T(8,128)(2,1)}, u32[]{:S(2)}) copy-start(bf16[8,4096]{1,0:T(8,128)(2,1)} %state_hbm.1) | copy-start | bytes 196612
  4.8 0.8 %copy-start.2 = (bf16[12,1024]{1,0:T(8,128)(2,1)S(1)}, bf16[12,1024]{1,0:T(8,128)(2,1)}, u32[]{:S(2)}) copy-start(bf16[12,1024]{1,0:T(8,128)(2,1)} %flux_hbm.1) | copy-start | bytes 73732
  5.6 0.7 %copy-start.3 = (f32[4096]{0:T(1024)S(1)}, f32[4096]{0:T(1024)}, u32[]{:S(2)}) copy-start(f32[4096]{0:T(1024)} %param.11) | copy-start | bytes 49156
  6.3 0.7 %copy-start.4 = (s32[1,3,4,6]{3,2,1,0:T(4,128)S(1)}, s32[1,3,4,6]{3,2,1,0:T(4,128)}, u32[]{:S(2)}) copy-start(s32[1,3,4,6]{3,2,1,0:T(4,128)} %block_hbm.1) | copy-start | bytes 868
  7.0 0.7 %copy-start.5 = (f32[1024]{0:T(1024)S(1)}, f32[1024]{0:T(1024)}, u32[]{:S(2)}) copy-start(f32[1024]{0:T(1024)} %param.13) | copy-start | bytes 12292
  7.7 0.7 %copy-start.6 = (s32[8,12]{1,0:T(8,128)S(1)}, s32[8,12]{1,0:T(8,128)}, u32[]{:S(2)}) copy-start(s32[8,12]{1,0:T(8,128)} %link_slot_hbm.1) | copy-start | bytes 1156
  8.4 0.7 %copy-start.7 = (s32[8]{0:T(128)S(1)}, s32[8]{0:T(128)}, u32[]{:S(2)}) copy-start(s32[8]{0:T(128)} %link_count_hbm.1) | copy-start | bytes 100

commit v2 on v1

--- a/solution.py
+++ b/solution.py
@@ -9,6 +9,7 @@
 from jax.sharding import PartitionSpec as P
 
 MESH = pl.DeviceIdType.MESH
+VMEM_BYTES = 60 * 1024 * 1024
 
 
 def kernel(
@@ -25,9 +26,11 @@
     count_hbm,
     link_slot_hbm,
     link_count_hbm,
+    state_out_hbm,
+    flux_out_hbm,
+    imbalance_out,
     state_out,
     flux_out,
-    imbalance_out,
     state_in,
     ocean_area_in,
     flux_in,
@@ -38,6 +41,8 @@
     count_in,
     link_slot_in,
     link_count_in,
+    picked,
+    read_slot,
     state_wide,
     state_send,
     state_recv,
@@ -59,7 +64,7 @@
     grp_sems,
 ):
     f32, bf16, i32 = jnp.float32, jnp.bfloat16, jnp.int32
-    ocean_blocks = state_wide.shape[0]
+    ocean_blocks = ocean_area_hbm.shape[0]
     fields_ocean = state_wide.shape[1]
     width = state_wide.shape[2]
     fields_atm = flux_in.shape[0]
@@ -76,7 +81,7 @@
         (block_hbm, block_in),
         (count_hbm, count_in),
         (state_hbm, state_in),
-        (ocean_area_hbm, ocean_area_in),
+        (ocean_area_hbm, ocean_area_in.at[pl.ds(0, ocean_area_hbm.shape[0])]),
         (link_slot_hbm, link_slot_in),
         (link_count_hbm, link_count_in),
         (coupling_hbm, coupling_in),
@@ -120,40 +125,43 @@
         loads[n].wait()
     for b in range(ocean_blocks):
         state_wide[b] = state_in[:, b * width : (b + 1) * width].astype(f32)
-
-    def alive(o, k, c):
-        return jnp.where(c < count_in[0, o, k], 1.0, 0.0).astype(f32)
-
-    def fill_state(o, t):
-        k = sub_at(t)
-        rows = [
-            state_wide[block_in[0, o, k, c]] * alive(o, k, c) for c in range(capacity)
-        ]
-        return jnp.concatenate(rows, axis=0).astype(bf16)
+    state_wide[ocean_blocks] = jnp.zeros((fields_ocean, width), f32)
+
+    def block_at(o, k, c):
+        return jnp.where(c < count_in[o, 0, k], block_in[0, o, k, c], ocean_blocks)
+
+    for o in range(3):
+        for k in range(subs):
+            for c in range(capacity):
+                picked[(o * subs + k) * capacity + c] = block_at(o, k, c)
 
     state_copies = []
-    for n, (o, t) in enumerate(steps):
-        state_send[o * subs + sub_at(t)] = fill_state(o, t)
-        if n == 0:
+    for o in (0, 2, 1):
+        for k in range(subs):
+            first = (o * subs + k) * capacity
+            rows = [state_wide[picked[first + c]] for c in range(capacity)]
+            state_send[o * subs + k] = jnp.concatenate(rows, axis=0).astype(bf16)
+        if o == 0:
             pl.semaphore_wait(barrier, len(partners))
-        copy = exchange(state_send, state_recv, state_sems, o, t)
-        copy.start()
-        state_copies.append(copy)
-    state_recv[subs + me_sub] = fill_state(1, 0)
+        for t in range(1 if o == 1 else 0, subs):
+            copy = exchange(state_send, state_recv, state_sems, o, t)
+            copy.start()
+            state_copies.append(copy)
+    state_recv[subs + me_sub] = state_send[subs + me_sub]
 
     loads[3].wait()
+    ocean_area_in[ocean_blocks] = jnp.zeros((1, width), f32)
     area_copies = []
-    for o, t in steps + [(1, 0)]:
-        k = sub_at(t)
-        target = area_recv if (o, t) == (1, 0) else area_send
-        for c in range(capacity):
-            target[o * subs + k, c : c + 1, :] = ocean_area_in[block_in[0, o, k, c]] * alive(
-                o, k, c
-            )
-        if (o, t) != (1, 0):
+    for o in (0, 2, 1):
+        for k in range(subs):
+            p = o * subs + k
+            for c in range(capacity):
+                area_send[p, c : c + 1, :] = ocean_area_in[picked[p * capacity + c]]
+        for t in range(1 if o == 1 else 0, subs):
             copy = exchange(area_send, area_recv, area_sems, o, t)
             copy.start()
             area_copies.append(copy)
+    area_recv[subs + me_sub] = area_send[subs + me_sub]
 
     for n in range(4, 9):
         loads[n].wait()
@@ -164,8 +172,10 @@
     for a in range(atm_blocks):
         for l in range(link_total):
             slot = link_slot_in[a, l]
+            used = l < link_count_in[a]
+            read_slot[a * link_total + l] = jnp.where(used, slot, routes * capacity)
             row = (slot // capacity) * quad_rows + slot % capacity
-            row = jnp.where(l < link_count_in[a], row, -quad_rows)
+            row = jnp.where(used, row, -quad_rows)
             key = jnp.where(link_of == a * link_total + l, row, key)
     key = key + quad_of * capacity
     key = jnp.where(key < 0, -1, key)
@@ -179,7 +189,7 @@
     for o in range(3):
         for k in range(subs):
             for c in range(capacity):
-                block = jnp.where(c < count_in[0, o, k], block_in[0, o, k, c] * 16, -32)
+                block = jnp.where(c < count_in[o, 0, k], block_in[0, o, k, c] * 16, -32)
                 key = jnp.where(slot_of == (o * subs + k) * capacity + c, block, key)
     key = key + inner // capacity
     key = jnp.where(inner < fields_atm * capacity, key, -1)
@@ -189,10 +199,14 @@
         chooser[part * rows : (part + 1) * rows, :] = jnp.where(row_of == key, 1.0, 0.0).astype(
             bf16
         )
-    coefficient = [
-        jnp.broadcast_to(coupling_in[:, f : f + 1], (fields_atm, width))
-        for f in range(fields_ocean)
-    ]
+    row_of = lax.broadcasted_iota(i32, (fields_atm, fields_atm), 0)
+    lane_of = lax.broadcasted_iota(i32, (fields_atm, fields_atm), 1)
+    arrived[routes * capacity] = jnp.zeros((fields_ocean, width), f32)
+    coefficient = []
+    for f in range(fields_ocean):
+        spread = jnp.where(row_of == lane_of, coupling_in[f : f + 1, :], 0.0)
+        column = jnp.sum(spread, axis=1, keepdims=True)
+        coefficient.append(jnp.broadcast_to(column, (fields_atm, width)))
 
     for copy in state_copies:
         copy.wait_recv()
@@ -204,10 +218,7 @@
 
     atm_acc = jnp.zeros((fields_atm, width), f32)
     for a in range(atm_blocks):
-        taken = []
-        for l in range(link_total):
-            used = jnp.where(l < link_count_in[a], 1.0, 0.0).astype(f32)
-            taken.append(arrived[link_slot_in[a, l]] * used)
+        taken = [arrived[read_slot[a * link_total + l]] for l in range(link_total)]
         taken = jnp.concatenate(taken, axis=1).astype(bf16)
         weight = weight_in[a].reshape(link_total * width, width)
         state_sum = jnp.dot(taken, weight, preferred_element_type=f32)
@@ -226,6 +237,9 @@
             parts[pl.ds(a * link_total + l, fields_atm, stride=links), :] = part[
                 :, l * width : (l + 1) * width
             ]
+
+    state_store = pltpu.make_async_copy(state_out, state_out_hbm, load_sem.at[10])
+    state_store.start()
 
     quads = []
     for q in range(fields_atm // 4):
@@ -262,7 +276,7 @@
     mine = to_lanes(jnp.sum(atm_acc, axis=1, keepdims=True), 1) - to_lanes(
         jnp.sum(ocean_rows, axis=1, keepdims=True), capacity
     )
-    sub_parts[me_sub] = jnp.broadcast_to(mine, (8, 128))
+    sub_parts[me_sub] = mine
     sub_copies = []
     for t in range(1, subs):
         copy = pltpu.make_async_remote_copy(
@@ -303,6 +317,9 @@
             b * 16 : b * 16 + fields_atm
         ].astype(bf16)
 
+    flux_store = pltpu.make_async_copy(flux_out, flux_out_hbm, load_sem.at[11])
+    flux_store.start()
+
     for copy in grp_copies:
         copy.wait_recv()
     total = grp_parts[0]
@@ -311,6 +328,20 @@
     imbalance_out[...] = total * norm_scale
     for copy in state_copies + area_copies + flux_copies + sub_copies + grp_copies:
         copy.wait_send()
+    state_store.wait()
+    flux_store.wait()
+
+
+def finish(state_in, flux_in, total_in, state_out, flux_out, total_out, sems):
+    copies = [
+        pltpu.make_async_copy(flux_in, flux_out, sems.at[0]),
+        pltpu.make_async_copy(state_in, state_out, sems.at[1]),
+    ]
+    for copy in copies:
+        copy.start()
+    total_out[...] = total_in[0, : total_out.shape[0]]
+    for copy in copies:
+        copy.wait()
 
 
 def shards(
@@ -344,25 +375,29 @@
         out_shape=(
             jax.ShapeDtypeStruct((fields_ocean, atm_blocks * width), bf16),
             jax.ShapeDtypeStruct((fields_atm, ocean_blocks * width), bf16),
-            jax.ShapeDtypeStruct((8, 128), f32),
+            jax.ShapeDtypeStruct((1, 128), f32),
         ),
         in_specs=[anywhere] * 10,
-        out_specs=(vmem, vmem, vmem),
+        out_specs=(anywhere, anywhere, vmem),
         scratch_shapes=[
+            pltpu.VMEM((fields_ocean, atm_blocks * width), bf16),
+            pltpu.VMEM((fields_atm, ocean_blocks * width), bf16),
             pltpu.VMEM(ocean_state.shape, bf16),
-            pltpu.VMEM((ocean_blocks, 1, width), f32),
+            pltpu.VMEM((ocean_blocks + 1, 1, width), f32),
             pltpu.VMEM(atm_flux.shape, bf16),
             pltpu.VMEM((atm_blocks, width), f32),
-            pltpu.VMEM(coupling.shape, f32),
+            pltpu.VMEM((fields_ocean, fields_atm), f32),
             pltpu.VMEM(remap_weight.shape, bf16),
             pltpu.SMEM(send_block.shape, i32),
-            pltpu.SMEM(send_count.shape, i32),
+            pltpu.SMEM((3, 1, subs), i32),
             pltpu.SMEM(link_slot.shape, i32),
             pltpu.SMEM(link_count.shape, i32),
-            pltpu.VMEM((ocean_blocks, fields_ocean, width), f32),
+            pltpu.SMEM((routes * capacity,), i32),
+            pltpu.SMEM((links,), i32),
+            pltpu.VMEM((ocean_blocks + 1, fields_ocean, width), f32),
             pltpu.VMEM((routes, capacity * fields_ocean, width), bf16),
             pltpu.VMEM((routes, capacity * fields_ocean, width), bf16),
-            pltpu.VMEM((routes * capacity, fields_ocean, width), f32),
+            pltpu.VMEM((routes * capacity + 1, fields_ocean, width), f32),
             pltpu.VMEM((routes, 8, width), f32),
             pltpu.VMEM((routes, 8, width), f32),
             pltpu.VMEM((fields_atm * links, width), f32),
@@ -370,9 +405,9 @@
             pltpu.VMEM((ocean_blocks * 16, routes * flux_rows), bf16),
             pltpu.VMEM((routes, flux_rows, width), bf16),
             pltpu.VMEM((routes, flux_rows, width), bf16),
-            pltpu.VMEM((subs, 8, 128), f32),
-            pltpu.VMEM((groups, 8, 128), f32),
-            pltpu.SemaphoreType.DMA((10,)),
+            pltpu.VMEM((subs, 1, 128), f32),
+            pltpu.VMEM((groups, 1, 128), f32),
+            pltpu.SemaphoreType.DMA((12,)),
             pltpu.SemaphoreType.DMA((2, 3, subs)),
             pltpu.SemaphoreType.DMA((2, 3, subs)),
             pltpu.SemaphoreType.DMA((2, 3, subs)),
@@ -380,21 +415,32 @@
             pltpu.SemaphoreType.DMA((2, groups)),
         ],
         compiler_params=pltpu.CompilerParams(
-            collective_id=0, has_side_effects=True, vmem_limit_bytes=40 * 1024 * 1024
+            collective_id=0, has_side_effects=True, vmem_limit_bytes=VMEM_BYTES
         ),
     )(
         ocean_state,
         ocean_area.reshape(ocean_blocks, 1, width),
         atm_flux,
         atm_area.reshape(atm_blocks, width),
-        coupling,
+        coupling.T,
         remap_weight,
         send_block,
-        send_count,
+        send_count.reshape(3, 1, subs),
         link_slot,
         link_count,
     )
-    return state_on_atm, flux_on_ocean, imbalance[0, :fields_atm]
+    return pl.pallas_call(
+        finish,
+        out_shape=(
+            jax.ShapeDtypeStruct(state_on_atm.shape, bf16),
+            jax.ShapeDtypeStruct(flux_on_ocean.shape, bf16),
+            jax.ShapeDtypeStruct((fields_atm,), f32),
+        ),
+        in_specs=[anywhere, anywhere, vmem],
+        out_specs=(anywhere, anywhere, vmem),
+        scratch_shapes=[pltpu.SemaphoreType.DMA((2,))],
+        compiler_params=pltpu.CompilerParams(vmem_limit_bytes=VMEM_BYTES),
+    )(state_on_atm, flux_on_ocean, imbalance)
 
 
 def solution(mesh):

time: 35.4 us -> 31.3 us (0.88)
  local copies, waits for them, and re-layouts: 10.1 us -> 0 us
  Pallas kernels: 24.1 us -> 30.5 us
    unnamed x20 -> x0, local copies, waits for them, and re-layouts: 9.63 us -> none
    pallas_call x0 -> x1, Pallas kernels: none -> 6.75 us  [shards(): pl.pallas_call(finish, out_shape=(jax.ShapeDtypeStruct(state_on_atm.shape...]
    squeeze x1 -> x0, local copies, waits for them, and re-layouts: 0.51 us -> none  [shards(): return (state_on_atm, flux_on_ocean, imbalance[0, :fields_atm])]
    pallas_call x1, Pallas kernels: 24.1 us -> 23.7 us  [shards(): pl.pallas_call(functools.partial(kernel, groups, subs, norm_scale), out_s...]
where the time goes in v2:
time: 31.3 us; the launch traced here: 31.1 us
  Pallas kernels  30.5 us (97%)
  between operations  0.64 us (2%)
    pallas_call x1, Pallas kernels, shards(): pl.pallas_call(functools.partial(kernel, groups, subs, norm_scale), out_s...  23.7 us
    pallas_call x1, Pallas kernels, shards(): pl.pallas_call(finish, out_shape=(jax.ShapeDtypeStruct(state_on_atm.shape...  6.75 us

profile of v2, /device:TPU:0, one launch (start us, length us, event | category | flops | bytes accessed | tf_op | source)
XLA Modules:
  0.0 31.1 jit_solution(10903051466190033974)
XLA Ops:
  0.6 23.7 %shard_map.121 = (bf16[8,1024]{1,0:T(8,128)(2,1)}, bf16[12,4096]{1,0:T(8,128)(2,1)}, f32[1,128]{1,0:T(1,128)}) custom-call(bf16[8,4096]{1,0:T(8,128)(2,1)} %state_hbm.1, f32[32,1,128]{2,1,0:T(1,128)} %bitcast.4, bf16[12,1024]{1,0:T(8,128)(2,1)} %flux_hbm.1, f32[8,128]{1,0:T(8,128)} %bitcast.5, f32[8,12]{1,0:T(8,128)} %bitcast.6, ...), custom_call_target="tpu_custom_call" | custom-call | tf_op jit(solution)/shard_map/pallas_call | solution.py:373
  24.4 6.7 %shard_map.122 = (bf16[8,1024]{1,0:T(8,128)(2,1)}, bf16[12,4096]{1,0:T(8,128)(2,1)}, f32[12]{0:T(128)}) custom-call(bf16[8,1024]{1,0:T(8,128)(2,1)} %get-tuple-element.6.state_in, bf16[12,4096]{1,0:T(8,128)(2,1)} %get-tuple-element.7.flux_in, f32[1,128]{1,0:T(1,128)} %get-tuple-element.8.total_in), custom_call_target="tpu_custom_call" | custom-call | tf_op jit(solution)/shard_map/pallas_call | solution.py:432

commit v3 on v2

--- a/solution.py
+++ b/solution.py
@@ -26,11 +26,9 @@
     count_hbm,
     link_slot_hbm,
     link_count_hbm,
-    state_out_hbm,
-    flux_out_hbm,
-    imbalance_out,
     state_out,
     flux_out,
+    imbalance_out,
     state_in,
     ocean_area_in,
     flux_in,
@@ -238,9 +236,6 @@
                 :, l * width : (l + 1) * width
             ]
 
-    state_store = pltpu.make_async_copy(state_out, state_out_hbm, load_sem.at[10])
-    state_store.start()
-
     quads = []
     for q in range(fields_atm // 4):
         operand = parts[q * 4 * links : (q + 1) * 4 * links, :].astype(bf16)
@@ -317,9 +312,6 @@
             b * 16 : b * 16 + fields_atm
         ].astype(bf16)
 
-    flux_store = pltpu.make_async_copy(flux_out, flux_out_hbm, load_sem.at[11])
-    flux_store.start()
-
     for copy in grp_copies:
         copy.wait_recv()
     total = grp_parts[0]
@@ -328,8 +320,6 @@
     imbalance_out[...] = total * norm_scale
     for copy in state_copies + area_copies + flux_copies + sub_copies + grp_copies:
         copy.wait_send()
-    state_store.wait()
-    flux_store.wait()
 
 
 def finish(state_in, flux_in, total_in, state_out, flux_out, total_out, sems):
@@ -373,15 +363,13 @@
     state_on_atm, flux_on_ocean, imbalance = pl.pallas_call(
         functools.partial(kernel, groups, subs, norm_scale),
         out_shape=(
-            jax.ShapeDtypeStruct((fields_ocean, atm_blocks * width), bf16),
-            jax.ShapeDtypeStruct((fields_atm, ocean_blocks * width), bf16),
-            jax.ShapeDtypeStruct((1, 128), f32),
+            pltpu.VMEM((fields_ocean, atm_blocks * width), bf16),
+            pltpu.VMEM((fields_atm, ocean_blocks * width), bf16),
+            pltpu.VMEM((1, 128), f32),
         ),
         in_specs=[anywhere] * 10,
-        out_specs=(anywhere, anywhere, vmem),
+        out_specs=(vmem, vmem, vmem),
         scratch_shapes=[
-            pltpu.VMEM((fields_ocean, atm_blocks * width), bf16),
-            pltpu.VMEM((fields_atm, ocean_blocks * width), bf16),
             pltpu.VMEM(ocean_state.shape, bf16),
             pltpu.VMEM((ocean_blocks + 1, 1, width), f32),
             pltpu.VMEM(atm_flux.shape, bf16),
@@ -407,7 +395,7 @@
             pltpu.VMEM((routes, flux_rows, width), bf16),
             pltpu.VMEM((subs, 1, 128), f32),
             pltpu.VMEM((groups, 1, 128), f32),
-            pltpu.SemaphoreType.DMA((12,)),
+            pltpu.SemaphoreType.DMA((10,)),
             pltpu.SemaphoreType.DMA((2, 3, subs)),
             pltpu.SemaphoreType.DMA((2, 3, subs)),
             pltpu.SemaphoreType.DMA((2, 3, subs)),
@@ -436,10 +424,10 @@
             jax.ShapeDtypeStruct(flux_on_ocean.shape, bf16),
             jax.ShapeDtypeStruct((fields_atm,), f32),
         ),
-        in_specs=[anywhere, anywhere, vmem],
+        in_specs=[vmem, vmem, vmem],
         out_specs=(anywhere, anywhere, vmem),
         scratch_shapes=[pltpu.SemaphoreType.DMA((2,))],
-        compiler_params=pltpu.CompilerParams(vmem_limit_bytes=VMEM_BYTES),
+        compiler_params=pltpu.CompilerParams(vmem_limit_bytes=1024 * 1024),
     )(state_on_atm, flux_on_ocean, imbalance)
 
 

time: 31.3 us -> 25.2 us (0.81)
  Pallas kernels: 30.5 us -> 24.3 us
    pallas_call x1, Pallas kernels: 6.75 us -> 1.19 us  [shards(): pl.pallas_call(finish, out_shape=(jax.ShapeDtypeStruct(state_on_atm.shape...]
    pallas_call x1, Pallas kernels: 23.7 us -> 23.1 us  [shards(): pl.pallas_call(functools.partial(kernel, groups, subs, norm_scale), out_s...]
where the time goes in v3:
time: 25.2 us; the launch traced here: 25 us
  Pallas kernels  24.3 us (96%)
  between operations  0.64 us (3%)
    pallas_call x1, Pallas kernels, shards(): pl.pallas_call(functools.partial(kernel, groups, subs, norm_scale), out_s...  23.1 us
    pallas_call x1, Pallas kernels, shards(): pl.pallas_call(finish, out_shape=(jax.ShapeDtypeStruct(state_on_atm.shape...  1.19 us

profile of v3, /device:TPU:0, one launch (start us, length us, event | category | flops | bytes accessed | tf_op | source)
XLA Modules:
  0.0 25.0 jit_solution(5412238213058694254)
XLA Ops:
  0.6 23.1 %shard_map.121 = (bf16[8,1024]{1,0:T(8,128)(2,1)S(1)}, bf16[12,4096]{1,0:T(8,128)(2,1)S(1)}, f32[1,128]{1,0:T(1,128)S(1)}) custom-call(bf16[8,4096]{1,0:T(8,128)(2,1)} %state_hbm.1, f32[32,1,128]{2,1,0:T(1,128)} %bitcast.4, bf16[12,1024]{1,0:T(8,128)(2,1)} %flux_hbm.1, f32[8,128]{1,0:T(8,128)} %bitcast.5, f32[8,12]{1,0:T(8,128)} %bitcast.6, ...), custom_call_target="tpu_custom_call" | custom-call | tf_op jit(solution)/shard_map/pallas_call | solution.py:363
  23.8 1.2 %shard_map.122 = (bf16[8,1024]{1,0:T(8,128)(2,1)}, bf16[12,4096]{1,0:T(8,128)(2,1)}, f32[12]{0:T(128)}) custom-call(bf16[8,1024]{1,0:T(8,128)(2,1)S(1)} %get-tuple-element.6.state_in, bf16[12,4096]{1,0:T(8,128)(2,1)S(1)} %get-tuple-element.7.flux_in, f32[1,128]{1,0:T(1,128)S(1)} %get-tuple-element.8.total_in), custom_call_target="tpu_custom_call" | custom-call | tf_op jit(solution)/shard_map/pallas_call | solution.py:420

commit v4 on v3

--- a/solution.py
+++ b/solution.py
@@ -91,7 +91,7 @@
         pltpu.make_async_copy(source, target, load_sem.at[n])
         for n, (source, target) in enumerate(pairs)
     ]
-    for load in loads:
+    for load in loads[:3]:
         load.start()
 
     steps = [(o, t) for o in (0, 2) for t in range(subs)] + [(1, t) for t in range(1, subs)]
@@ -108,22 +108,31 @@
     for partner in partners:
         pl.semaphore_signal(barrier, inc=1, device_id=partner, device_id_type=MESH)
 
+    for load in loads[3:]:
+        load.start()
+
     def exchange(source, target, sems, o, t):
         k = sub_at(t)
         return pltpu.make_async_remote_copy(
             src_ref=source.at[o * subs + k],
             dst_ref=target.at[(2 - o) * subs + me_sub],
-            send_sem=sems.at[0, o, t],
-            recv_sem=sems.at[1, o, t],
+            send_sem=sems.at[0],
+            recv_sem=sems.at[1],
             device_id=(grp_at(o - 1), k),
             device_id_type=MESH,
         )
 
-    for n in range(3):
-        loads[n].wait()
+    def drain(buffer, sem, count):
+        ref = buffer.at[pl.ds(0, count)]
+        pltpu.make_async_copy(ref, ref, sem).wait()
+
+    loads[2].wait()
     for b in range(ocean_blocks):
         state_wide[b] = state_in[:, b * width : (b + 1) * width].astype(f32)
     state_wide[ocean_blocks] = jnp.zeros((fields_ocean, width), f32)
+
+    loads[0].wait()
+    loads[1].wait()
 
     def block_at(o, k, c):
         return jnp.where(c < count_in[o, 0, k], block_in[0, o, k, c], ocean_blocks)
@@ -133,7 +142,6 @@
             for c in range(capacity):
                 picked[(o * subs + k) * capacity + c] = block_at(o, k, c)
 
-    state_copies = []
     for o in (0, 2, 1):
         for k in range(subs):
             first = (o * subs + k) * capacity
@@ -142,23 +150,18 @@
         if o == 0:
             pl.semaphore_wait(barrier, len(partners))
         for t in range(1 if o == 1 else 0, subs):
-            copy = exchange(state_send, state_recv, state_sems, o, t)
-            copy.start()
-            state_copies.append(copy)
+            exchange(state_send, state_recv, state_sems, o, t).start()
     state_recv[subs + me_sub] = state_send[subs + me_sub]
 
     loads[3].wait()
     ocean_area_in[ocean_blocks] = jnp.zeros((1, width), f32)
-    area_copies = []
     for o in (0, 2, 1):
         for k in range(subs):
             p = o * subs + k
             for c in range(capacity):
                 area_send[p, c : c + 1, :] = ocean_area_in[picked[p * capacity + c]]
         for t in range(1 if o == 1 else 0, subs):
-            copy = exchange(area_send, area_recv, area_sems, o, t)
-            copy.start()
-            area_copies.append(copy)
+            exchange(area_send, area_recv, area_sems, o, t).start()
     area_recv[subs + me_sub] = area_send[subs + me_sub]
 
     for n in range(4, 9):
@@ -180,6 +183,111 @@
     row_of = lax.broadcasted_iota(i32, (routes * quad_rows, 4 * links), 0)
     slot_hits[...] = jnp.where(row_of == key, 1.0, 0.0).astype(bf16)
 
+    row_of = lax.broadcasted_iota(i32, (16, fields_atm), 0)
+    lane_of = lax.broadcasted_iota(i32, (16, fields_atm), 1)
+    arrived[routes * capacity] = jnp.zeros((fields_ocean, width), f32)
+    coefficient = []
+    for f in range(fields_ocean):
+        spread = jnp.where(row_of == lane_of, coupling_in[f : f + 1, :], 0.0)
+        column = jnp.sum(spread, axis=1, keepdims=True)
+        coefficient.append(jnp.broadcast_to(column, (16, width)))
+
+    drain(state_recv, state_sems.at[1], len(steps))
+    loads[9].wait()
+    for p in range(routes):
+        arrived[p * capacity : (p + 1) * capacity] = (
+            state_recv[p].astype(f32).reshape(capacity, fields_ocean, width)
+        )
+
+    pairs = [(a, a + 1) for a in range(0, atm_blocks, 2)]
+
+    def weight_of(pair):
+        return jnp.concatenate(
+            [weight_in[a].reshape(link_total * width, width) for a in pair], axis=1
+        )
+
+    sums = []
+    for pair in pairs:
+        taken = [
+            jnp.concatenate([arrived[read_slot[a * link_total + l]] for a in pair], axis=0)
+            for l in range(link_total)
+        ]
+        taken = jnp.concatenate(taken, axis=1).astype(bf16)
+        both = jnp.dot(taken, weight_of(pair), preferred_element_type=f32)
+        for n in range(2):
+            sums.append(both[n * fields_ocean : (n + 1) * fields_ocean, n * width : (n + 1) * width])
+
+    atm_acc = jnp.zeros((16, width), f32)
+    margin = jnp.zeros((16 - fields_atm, width), f32)
+    coupled = []
+    for a, state_sum in enumerate(sums):
+        here = slice(a * width, (a + 1) * width)
+        state_out[:, here] = state_sum.astype(bf16)
+        change = coefficient[0] * state_sum[0:1]
+        for f in range(1, fields_ocean):
+            change = change + coefficient[f] * state_sum[f : f + 1]
+        value = jnp.concatenate([flux_in[:, here].astype(f32), margin], axis=0)
+        coupled.append((value + change).astype(bf16))
+        atm_acc = atm_acc + atm_area_in[a : a + 1, :] * coupled[a].astype(f32)
+
+    none = jnp.zeros((16, width), bf16)
+    for pair in pairs:
+        left = jnp.concatenate([coupled[pair[0]], none], axis=0)
+        right = jnp.concatenate([none, coupled[pair[1]]], axis=0)
+        part = lax.dot_general(
+            jnp.concatenate([left, right], axis=1),
+            weight_of(pair),
+            (((1,), (1,)), ((), ())),
+            preferred_element_type=f32,
+        )
+        for n, a in enumerate(pair):
+            for l in range(link_total):
+                parts[pl.ds(a * link_total + l, fields_atm, stride=links), :] = part[
+                    n * 16 : n * 16 + fields_atm, l * width : (l + 1) * width
+                ]
+
+    quads = []
+    for q in range(fields_atm // 4):
+        operand = parts[q * 4 * links : (q + 1) * 4 * links, :].astype(bf16)
+        quads.append(jnp.dot(slot_hits[...], operand, preferred_element_type=f32))
+    blank = jnp.zeros((flux_rows - fields_atm * capacity, width), f32)
+    for p in range(routes):
+        rows = [quad[p * quad_rows : (p + 1) * quad_rows] for quad in quads]
+        flux_send[p] = jnp.concatenate(rows + [blank], axis=0).astype(bf16)
+    for o, t in steps:
+        exchange(flux_send, flux_recv, flux_sems, o, t).start()
+    flux_recv[subs + me_sub] = flux_send[subs + me_sub]
+
+    drain(area_recv, area_sems.at[1], len(steps))
+    ocean_acc = [jnp.zeros((quad_rows, width), f32) for _ in quads]
+    for p in range(routes):
+        area = area_recv[p][:capacity]
+        area = jnp.concatenate([area] * 4, axis=0)
+        for q, quad in enumerate(quads):
+            rounded = quad[p * quad_rows : (p + 1) * quad_rows].astype(bf16).astype(f32)
+            ocean_acc[q] = ocean_acc[q] + rounded * area
+
+    def to_lanes(column, group):
+        rows = column.shape[0]
+        row_of = lax.broadcasted_iota(i32, (rows, 128), 0) // group
+        lane_of = lax.broadcasted_iota(i32, (rows, 128), 1)
+        return jnp.sum(jnp.where(row_of == lane_of, column, 0.0), axis=0, keepdims=True)
+
+    ocean_rows = jnp.concatenate(ocean_acc, axis=0)
+    mine = to_lanes(jnp.sum(atm_acc, axis=1, keepdims=True), 1) - to_lanes(
+        jnp.sum(ocean_rows, axis=1, keepdims=True), capacity
+    )
+    sub_parts[me_sub] = mine
+    for t in range(1, subs):
+        copy = pltpu.make_async_remote_copy(
+            src_ref=sub_parts.at[me_sub],
+            dst_ref=sub_parts.at[me_sub],
+            send_sem=sub_sems.at[0],
+            recv_sem=sub_sems.at[1],
+            device_id=(me_grp, sub_at(t)),
+            device_id_type=MESH,
+        )
+        copy.start()
     lane = lax.broadcasted_iota(i32, (1, routes * flux_rows), 1)
     inner = lane % flux_rows
     slot_of = (lane // flux_rows) * capacity + inner % capacity
@@ -197,114 +305,26 @@
         chooser[part * rows : (part + 1) * rows, :] = jnp.where(row_of == key, 1.0, 0.0).astype(
             bf16
         )
-    row_of = lax.broadcasted_iota(i32, (fields_atm, fields_atm), 0)
-    lane_of = lax.broadcasted_iota(i32, (fields_atm, fields_atm), 1)
-    arrived[routes * capacity] = jnp.zeros((fields_ocean, width), f32)
-    coefficient = []
-    for f in range(fields_ocean):
-        spread = jnp.where(row_of == lane_of, coupling_in[f : f + 1, :], 0.0)
-        column = jnp.sum(spread, axis=1, keepdims=True)
-        coefficient.append(jnp.broadcast_to(column, (fields_atm, width)))
-
-    for copy in state_copies:
-        copy.wait_recv()
-    loads[9].wait()
-    for p in range(routes):
-        arrived[p * capacity : (p + 1) * capacity] = (
-            state_recv[p].astype(f32).reshape(capacity, fields_ocean, width)
-        )
-
-    atm_acc = jnp.zeros((fields_atm, width), f32)
-    for a in range(atm_blocks):
-        taken = [arrived[read_slot[a * link_total + l]] for l in range(link_total)]
-        taken = jnp.concatenate(taken, axis=1).astype(bf16)
-        weight = weight_in[a].reshape(link_total * width, width)
-        state_sum = jnp.dot(taken, weight, preferred_element_type=f32)
-        here = slice(a * width, (a + 1) * width)
-        state_out[:, here] = state_sum.astype(bf16)
-        value = flux_in[:, here].astype(f32)
-        change = coefficient[0] * state_sum[0:1]
-        for f in range(1, fields_ocean):
-            change = change + coefficient[f] * state_sum[f : f + 1]
-        coupled = (value + change).astype(bf16)
-        atm_acc = atm_acc + atm_area_in[a : a + 1, :] * coupled.astype(f32)
-        part = lax.dot_general(
-            coupled, weight, (((1,), (1,)), ((), ())), preferred_element_type=f32
-        )
-        for l in range(link_total):
-            parts[pl.ds(a * link_total + l, fields_atm, stride=links), :] = part[
-                :, l * width : (l + 1) * width
-            ]
-
-    quads = []
-    for q in range(fields_atm // 4):
-        operand = parts[q * 4 * links : (q + 1) * 4 * links, :].astype(bf16)
-        quads.append(jnp.dot(slot_hits[...], operand, preferred_element_type=f32))
-    blank = jnp.zeros((flux_rows - fields_atm * capacity, width), f32)
-    for p in range(routes):
-        rows = [quad[p * quad_rows : (p + 1) * quad_rows] for quad in quads]
-        flux_send[p] = jnp.concatenate(rows + [blank], axis=0).astype(bf16)
-    flux_copies = []
-    for o, t in steps:
-        copy = exchange(flux_send, flux_recv, flux_sems, o, t)
-        copy.start()
-        flux_copies.append(copy)
-    flux_recv[subs + me_sub] = flux_send[subs + me_sub]
-
-    for copy in area_copies:
-        copy.wait_recv()
-    ocean_acc = [jnp.zeros((quad_rows, width), f32) for _ in quads]
-    for p in range(routes):
-        area = area_recv[p][:capacity]
-        area = jnp.concatenate([area] * 4, axis=0)
-        for q, quad in enumerate(quads):
-            rounded = quad[p * quad_rows : (p + 1) * quad_rows].astype(bf16).astype(f32)
-            ocean_acc[q] = ocean_acc[q] + rounded * area
-
-    def to_lanes(column, group):
-        rows = column.shape[0]
-        row_of = lax.broadcasted_iota(i32, (rows, 128), 0) // group
-        lane_of = lax.broadcasted_iota(i32, (rows, 128), 1)
-        return jnp.sum(jnp.where(row_of == lane_of, column, 0.0), axis=0, keepdims=True)
-
-    ocean_rows = jnp.concatenate(ocean_acc, axis=0)
-    mine = to_lanes(jnp.sum(atm_acc, axis=1, keepdims=True), 1) - to_lanes(
-        jnp.sum(ocean_rows, axis=1, keepdims=True), capacity
-    )
-    sub_parts[me_sub] = mine
-    sub_copies = []
-    for t in range(1, subs):
-        copy = pltpu.make_async_remote_copy(
-            src_ref=sub_parts.at[me_sub],
-            dst_ref=sub_parts.at[me_sub],
-            send_sem=sub_sems.at[0, t],
-            recv_sem=sub_sems.at[1, t],
-            device_id=(me_grp, sub_at(t)),
-            device_id_type=MESH,
-        )
-        copy.start()
-        sub_copies.append(copy)
-    for copy in sub_copies:
-        copy.wait_recv()
+    drain(sub_parts, sub_sems.at[1], subs - 1)
     total = sub_parts[0]
     for k in range(1, subs):
         total = total + sub_parts[k]
     grp_parts[me_grp] = total
-    grp_copies = []
     for d in range(1, groups):
         copy = pltpu.make_async_remote_copy(
             src_ref=grp_parts.at[me_grp],
             dst_ref=grp_parts.at[me_grp],
-            send_sem=grp_sems.at[0, d],
-            recv_sem=grp_sems.at[1, d],
+            send_sem=grp_sems.at[0],
+            recv_sem=grp_sems.at[1],
             device_id=(grp_at(d), me_sub),
             device_id_type=MESH,
         )
         copy.start()
-        grp_copies.append(copy)
-
-    for copy in flux_copies:
-        copy.wait_recv()
+    drain(state_send, state_sems.at[0], len(steps))
+    drain(area_send, area_sems.at[0], len(steps))
+    drain(sub_parts, sub_sems.at[0], subs - 1)
+
+    drain(flux_recv, flux_sems.at[1], len(steps))
     returned = flux_recv[...].reshape(routes * flux_rows, width)
     flux_sum = jnp.dot(chooser[...], returned, preferred_element_type=f32)
     for b in range(ocean_blocks):
@@ -312,14 +332,13 @@
             b * 16 : b * 16 + fields_atm
         ].astype(bf16)
 
-    for copy in grp_copies:
-        copy.wait_recv()
+    drain(grp_parts, grp_sems.at[1], groups - 1)
     total = grp_parts[0]
     for i in range(1, groups):
         total = total + grp_parts[i]
     imbalance_out[...] = total * norm_scale
-    for copy in state_copies + area_copies + flux_copies + sub_copies + grp_copies:
-        copy.wait_send()
+    drain(flux_send, flux_sems.at[0], len(steps))
+    drain(grp_parts, grp_sems.at[0], groups - 1)
 
 
 def finish(state_in, flux_in, total_in, state_out, flux_out, total_out, sems):
@@ -396,11 +415,11 @@
             pltpu.VMEM((subs, 1, 128), f32),
             pltpu.VMEM((groups, 1, 128), f32),
             pltpu.SemaphoreType.DMA((10,)),
-            pltpu.SemaphoreType.DMA((2, 3, subs)),
-            pltpu.SemaphoreType.DMA((2, 3, subs)),
-            pltpu.SemaphoreType.DMA((2, 3, subs)),
-            pltpu.SemaphoreType.DMA((2, subs)),
-            pltpu.SemaphoreType.DMA((2, groups)),
+            pltpu.SemaphoreType.DMA((2,)),
+            pltpu.SemaphoreType.DMA((2,)),
+            pltpu.SemaphoreType.DMA((2,)),
+            pltpu.SemaphoreType.DMA((2,)),
+            pltpu.SemaphoreType.DMA((2,)),
         ],
         compiler_params=pltpu.CompilerParams(
             collective_id=0, has_side_effects=True, vmem_limit_bytes=VMEM_BYTES

time: 25.2 us -> 23.6 us (0.937)
  Pallas kernels: 24.3 us -> 22.8 us
    pallas_call x1, Pallas kernels: 23.1 us -> 21.6 us  [shards(): pl.pallas_call(functools.partial(kernel, groups, subs, norm_scale), out_s...]
where the time goes in v4:
time: 23.6 us; the launch traced here: 23.4 us
  Pallas kernels  22.8 us (97%)
  between operations  0.64 us (3%)
    pallas_call x1, Pallas kernels, shards(): pl.pallas_call(functools.partial(kernel, groups, subs, norm_scale), out_s...  21.6 us
    pallas_call x1, Pallas kernels, shards(): pl.pallas_call(finish, out_shape=(jax.ShapeDtypeStruct(state_on_atm.shape...  1.19 us

profile of v4, /device:TPU:0, one launch (start us, length us, event | category | flops | bytes accessed | tf_op | source)
XLA Modules:
  0.0 23.4 jit_solution(1075100657790966396)
XLA Ops:
  0.6 21.6 %shard_map.121 = (bf16[8,1024]{1,0:T(8,128)(2,1)S(1)}, bf16[12,4096]{1,0:T(8,128)(2,1)S(1)}, f32[1,128]{1,0:T(1,128)S(1)}) custom-call(bf16[8,4096]{1,0:T(8,128)(2,1)} %state_hbm.1, f32[32,1,128]{2,1,0:T(1,128)} %bitcast.4, bf16[12,1024]{1,0:T(8,128)(2,1)} %flux_hbm.1, f32[8,128]{1,0:T(8,128)} %bitcast.5, f32[8,12]{1,0:T(8,128)} %bitcast.6, ...), custom_call_target="tpu_custom_call" | custom-call | tf_op jit(solution)/shard_map/pallas_call | solution.py:382
  22.3 1.2 %shard_map.122 = (bf16[8,1024]{1,0:T(8,128)(2,1)}, bf16[12,4096]{1,0:T(8,128)(2,1)}, f32[12]{0:T(128)}) custom-call(bf16[8,1024]{1,0:T(8,128)(2,1)S(1)} %get-tuple-element.6.state_in, bf16[12,4096]{1,0:T(8,128)(2,1)S(1)} %get-tuple-element.7.flux_in, f32[1,128]{1,0:T(1,128)S(1)} %get-tuple-element.8.total_in), custom_call_target="tpu_custom_call" | custom-call | tf_op jit(solution)/shard_map/pallas_call | solution.py:439

commit v5 on v4

--- a/solution.py
+++ b/solution.py
@@ -27,7 +27,8 @@
     link_slot_hbm,
     link_count_hbm,
     state_out,
-    flux_out,
+    returned_out,
+    chooser,
     imbalance_out,
     state_in,
     ocean_area_in,
@@ -49,7 +50,6 @@
     area_recv,
     parts,
     slot_hits,
-    chooser,
     flux_send,
     flux_recv,
     sub_parts,
@@ -70,6 +70,7 @@
     capacity = block_in.shape[3]
     routes = 3 * subs
     links = atm_blocks * link_total
+    pitch = links + 2
     quad_rows = 4 * capacity
     flux_rows = flux_send.shape[1]
     me_grp = lax.axis_index("grp")
@@ -166,10 +167,10 @@
 
     for n in range(4, 9):
         loads[n].wait()
-    lane = lax.broadcasted_iota(i32, (1, 4 * links), 1)
-    link_of = lane % links
-    quad_of = lane // links
-    key = jnp.full((1, 4 * links), -1, i32)
+    lane = lax.broadcasted_iota(i32, (1, 4 * pitch), 1)
+    link_of = lane % pitch
+    quad_of = lane // pitch
+    key = jnp.full((1, 4 * pitch), -quad_rows, i32)
     for a in range(atm_blocks):
         for l in range(link_total):
             slot = link_slot_in[a, l]
@@ -180,11 +181,13 @@
             key = jnp.where(link_of == a * link_total + l, row, key)
     key = key + quad_of * capacity
     key = jnp.where(key < 0, -1, key)
-    row_of = lax.broadcasted_iota(i32, (routes * quad_rows, 4 * links), 0)
+    row_of = lax.broadcasted_iota(i32, (routes * quad_rows, 4 * pitch), 0)
     slot_hits[...] = jnp.where(row_of == key, 1.0, 0.0).astype(bf16)
 
     row_of = lax.broadcasted_iota(i32, (16, fields_atm), 0)
     lane_of = lax.broadcasted_iota(i32, (16, fields_atm), 1)
+    for g in range(fields_atm):
+        parts[g * pitch + links : (g + 1) * pitch, :] = jnp.zeros((pitch - links, width), f32)
     arrived[routes * capacity] = jnp.zeros((fields_ocean, width), f32)
     coefficient = []
     for f in range(fields_ocean):
@@ -242,13 +245,13 @@
         )
         for n, a in enumerate(pair):
             for l in range(link_total):
-                parts[pl.ds(a * link_total + l, fields_atm, stride=links), :] = part[
+                parts[pl.ds(a * link_total + l, fields_atm, stride=pitch), :] = part[
                     n * 16 : n * 16 + fields_atm, l * width : (l + 1) * width
                 ]
 
     quads = []
     for q in range(fields_atm // 4):
-        operand = parts[q * 4 * links : (q + 1) * 4 * links, :].astype(bf16)
+        operand = parts[q * 4 * pitch : (q + 1) * 4 * pitch, :].astype(bf16)
         quads.append(jnp.dot(slot_hits[...], operand, preferred_element_type=f32))
     blank = jnp.zeros((flux_rows - fields_atm * capacity, width), f32)
     for p in range(routes):
@@ -325,12 +328,7 @@
     drain(sub_parts, sub_sems.at[0], subs - 1)
 
     drain(flux_recv, flux_sems.at[1], len(steps))
-    returned = flux_recv[...].reshape(routes * flux_rows, width)
-    flux_sum = jnp.dot(chooser[...], returned, preferred_element_type=f32)
-    for b in range(ocean_blocks):
-        flux_out[:, b * width : (b + 1) * width] = flux_sum[
-            b * 16 : b * 16 + fields_atm
-        ].astype(bf16)
+    returned_out[...] = flux_recv[...].reshape(routes * flux_rows, width)
 
     drain(grp_parts, grp_sems.at[1], groups - 1)
     total = grp_parts[0]
@@ -341,16 +339,34 @@
     drain(grp_parts, grp_sems.at[0], groups - 1)
 
 
-def finish(state_in, flux_in, total_in, state_out, flux_out, total_out, sems):
-    copies = [
-        pltpu.make_async_copy(flux_in, flux_out, sems.at[0]),
-        pltpu.make_async_copy(state_in, state_out, sems.at[1]),
-    ]
-    for copy in copies:
-        copy.start()
+def finish(
+    state_in, returned, chooser, total_in, state_out, flux_out, total_out, flux_sum, sems
+):
+    width = returned.shape[1]
+    fields_atm = flux_sum.shape[0]
+    store_state = pltpu.make_async_copy(state_in, state_out, sems.at[2])
+    store_state.start()
+    half = chooser.shape[0] // 2
+    blocks = half // 16
+    stores = []
+    for n in range(2):
+        block_sum = jnp.dot(
+            chooser[n * half : (n + 1) * half, :],
+            returned[...],
+            preferred_element_type=jnp.float32,
+        )
+        for b in range(blocks):
+            at = (n * blocks + b) * width
+            flux_sum[:, at : at + width] = block_sum[b * 16 : b * 16 + fields_atm].astype(
+                jnp.bfloat16
+            )
+        part = pl.ds(n * blocks * width, blocks * width)
+        store = pltpu.make_async_copy(flux_sum.at[:, part], flux_out.at[:, part], sems.at[n])
+        store.start()
+        stores.append(store)
     total_out[...] = total_in[0, : total_out.shape[0]]
-    for copy in copies:
-        copy.wait()
+    for store in stores + [store_state]:
+        store.wait()
 
 
 def shards(
@@ -375,19 +391,21 @@
     capacity = send_block.shape[3]
     routes = 3 * subs
     links = atm_blocks * link_total
+    pitch = links + 2
     flux_rows = -(-fields_atm * capacity // 16) * 16
     norm_scale = 1.0 / math.sqrt(groups * subs * atm_blocks * width)
     anywhere = pl.BlockSpec(memory_space=pl.ANY)
     vmem = pl.BlockSpec(memory_space=pltpu.VMEM)
-    state_on_atm, flux_on_ocean, imbalance = pl.pallas_call(
+    state_on_atm, returned, chooser, imbalance = pl.pallas_call(
         functools.partial(kernel, groups, subs, norm_scale),
         out_shape=(
             pltpu.VMEM((fields_ocean, atm_blocks * width), bf16),
-            pltpu.VMEM((fields_atm, ocean_blocks * width), bf16),
+            pltpu.VMEM((routes * flux_rows, width), bf16),
+            pltpu.VMEM((ocean_blocks * 16, routes * flux_rows), bf16),
             pltpu.VMEM((1, 128), f32),
         ),
         in_specs=[anywhere] * 10,
-        out_specs=(vmem, vmem, vmem),
+        out_specs=(vmem, vmem, vmem, vmem),
         scratch_shapes=[
             pltpu.VMEM(ocean_state.shape, bf16),
             pltpu.VMEM((ocean_blocks + 1, 1, width), f32),
@@ -407,9 +425,8 @@
             pltpu.VMEM((routes * capacity + 1, fields_ocean, width), f32),
             pltpu.VMEM((routes, 8, width), f32),
             pltpu.VMEM((routes, 8, width), f32),
-            pltpu.VMEM((fields_atm * links, width), f32),
-            pltpu.VMEM((routes * 4 * capacity, 4 * links), bf16),
-            pltpu.VMEM((ocean_blocks * 16, routes * flux_rows), bf16),
+            pltpu.VMEM((fields_atm * pitch, width), f32),
+            pltpu.VMEM((routes * 4 * capacity, 4 * pitch), bf16),
             pltpu.VMEM((routes, flux_rows, width), bf16),
             pltpu.VMEM((routes, flux_rows, width), bf16),
             pltpu.VMEM((subs, 1, 128), f32),
@@ -440,14 +457,17 @@
         finish,
         out_shape=(
             jax.ShapeDtypeStruct(state_on_atm.shape, bf16),
-            jax.ShapeDtypeStruct(flux_on_ocean.shape, bf16),
+            jax.ShapeDtypeStruct((fields_atm, ocean_blocks * width), bf16),
             jax.ShapeDtypeStruct((fields_atm,), f32),
         ),
-        in_specs=[vmem, vmem, vmem],
+        in_specs=[vmem] * 4,
         out_specs=(anywhere, anywhere, vmem),
-        scratch_shapes=[pltpu.SemaphoreType.DMA((2,))],
-        compiler_params=pltpu.CompilerParams(vmem_limit_bytes=1024 * 1024),
-    )(state_on_atm, flux_on_ocean, imbalance)
+        scratch_shapes=[
+            pltpu.VMEM((fields_atm, ocean_blocks * width), bf16),
+            pltpu.SemaphoreType.DMA((3,)),
+        ],
+        compiler_params=pltpu.CompilerParams(vmem_limit_bytes=8 * 1024 * 1024),
+    )(state_on_atm, returned, chooser, imbalance)
 
 
 def solution(mesh):

time: 23.6 us -> 24 us (1.017)
  Pallas kernels: 22.8 us -> 23.2 us
    pallas_call x1, Pallas kernels: 1.19 us -> 1.59 us  [shards(): pl.pallas_call(finish, out_shape=(jax.ShapeDtypeStruct(state_on_atm.shape...]
where the time goes in v5:
time: 24 us; the launch traced here: 23.8 us
  Pallas kernels  23.2 us (97%)
  between operations  0.64 us (3%)
    pallas_call x1, Pallas kernels, shards(): pl.pallas_call(functools.partial(kernel, groups, subs, norm_scale), out_s...  21.6 us
    pallas_call x1, Pallas kernels, shards(): pl.pallas_call(finish, out_shape=(jax.ShapeDtypeStruct(state_on_atm.shape...  1.59 us

profile of v5, /device:TPU:0, one launch (start us, length us, event | category | flops | bytes accessed | tf_op | source)
XLA Modules:
  0.0 23.8 jit_solution(7581916054994106159)
XLA Ops:
  0.6 21.6 %shard_map.121 = (bf16[8,1024]{1,0:T(8,128)(2,1)S(1)}, bf16[960,128]{1,0:T(8,128)(2,1)S(1)}, bf16[512,960]{1,0:T(8,128)(2,1)S(1)}, f32[1,128]{1,0:T(1,128)S(1)}) custom-call(bf16[8,4096]{1,0:T(8,128)(2,1)} %state_hbm.1, f32[32,1,128]{2,1,0:T(1,128)} %bitcast.4, bf16[12,1024]{1,0:T(8,128)(2,1)} %flux_hbm.1, f32[8,128]{1,0:T(8,128)} %bitcast.5, ...), custom_call_target="tpu_custom_call" | custom-call | tf_op jit(solution)/shard_map/pallas_call | solution.py:399
  22.3 1.6 %shard_map.122 = (bf16[8,1024]{1,0:T(8,128)(2,1)}, bf16[12,4096]{1,0:T(8,128)(2,1)}, f32[12]{0:T(128)}) custom-call(bf16[8,1024]{1,0:T(8,128)(2,1)S(1)} %get-tuple-element.7.state_in, bf16[960,128]{1,0:T(8,128)(2,1)S(1)} %get-tuple-element.8.returned, bf16[512,960]{1,0:T(8,128)(2,1)S(1)} %get-tuple-element.9.chooser, f32[1,128]{1,0:T(1,128)S(1)} %get-tuple-element.10.total_in), custom_call_target="tpu_custom_call" | custom-call | tf_op jit(solution)/shard_map/pallas_call | solution.py:456

commit v6 on v4

--- a/solution.py
+++ b/solution.py
@@ -52,14 +52,12 @@
     chooser,
     flux_send,
     flux_recv,
-    sub_parts,
-    grp_parts,
+    totals,
     load_sem,
     state_sems,
     area_sems,
     flux_sems,
-    sub_sems,
-    grp_sems,
+    total_sems,
 ):
     f32, bf16, i32 = jnp.float32, jnp.bfloat16, jnp.int32
     ocean_blocks = ocean_area_hbm.shape[0]
@@ -103,10 +101,19 @@
         return lax.rem(me_sub + t, subs)
 
     barrier = pltpu.get_barrier_semaphore()
-    partners = [(grp_at(o - 1), sub_at(t)) for o, t in steps]
-    partners += [(grp_at(d), me_sub) for d in range(2, groups - 1)]
-    for partner in partners:
+    others = groups * subs - 1
+
+    def each_other(visit):
+        def body(n, carry):
+            visit((grp_at(n // subs), sub_at(n % subs)))
+            return carry
+
+        lax.fori_loop(1, others + 1, body, 0, unroll=others < 64)
+
+    def greet(partner):
         pl.semaphore_signal(barrier, inc=1, device_id=partner, device_id_type=MESH)
+
+    each_other(greet)
 
     for load in loads[3:]:
         load.start()
@@ -148,7 +155,7 @@
             rows = [state_wide[picked[first + c]] for c in range(capacity)]
             state_send[o * subs + k] = jnp.concatenate(rows, axis=0).astype(bf16)
         if o == 0:
-            pl.semaphore_wait(barrier, len(partners))
+            pl.semaphore_wait(barrier, others)
         for t in range(1 if o == 1 else 0, subs):
             exchange(state_send, state_recv, state_sems, o, t).start()
     state_recv[subs + me_sub] = state_send[subs + me_sub]
@@ -277,17 +284,20 @@
     mine = to_lanes(jnp.sum(atm_acc, axis=1, keepdims=True), 1) - to_lanes(
         jnp.sum(ocean_rows, axis=1, keepdims=True), capacity
     )
-    sub_parts[me_sub] = mine
-    for t in range(1, subs):
-        copy = pltpu.make_async_remote_copy(
-            src_ref=sub_parts.at[me_sub],
-            dst_ref=sub_parts.at[me_sub],
-            send_sem=sub_sems.at[0],
-            recv_sem=sub_sems.at[1],
-            device_id=(me_grp, sub_at(t)),
+    me = me_grp * subs + me_sub
+    totals[me] = mine
+
+    def tell(partner):
+        pltpu.make_async_remote_copy(
+            src_ref=totals.at[me],
+            dst_ref=totals.at[me],
+            send_sem=total_sems.at[0],
+            recv_sem=total_sems.at[1],
+            device_id=partner,
             device_id_type=MESH,
-        )
-        copy.start()
+        ).start()
+
+    each_other(tell)
     lane = lax.broadcasted_iota(i32, (1, routes * flux_rows), 1)
     inner = lane % flux_rows
     slot_of = (lane // flux_rows) * capacity + inner % capacity
@@ -305,24 +315,8 @@
         chooser[part * rows : (part + 1) * rows, :] = jnp.where(row_of == key, 1.0, 0.0).astype(
             bf16
         )
-    drain(sub_parts, sub_sems.at[1], subs - 1)
-    total = sub_parts[0]
-    for k in range(1, subs):
-        total = total + sub_parts[k]
-    grp_parts[me_grp] = total
-    for d in range(1, groups):
-        copy = pltpu.make_async_remote_copy(
-            src_ref=grp_parts.at[me_grp],
-            dst_ref=grp_parts.at[me_grp],
-            send_sem=grp_sems.at[0],
-            recv_sem=grp_sems.at[1],
-            device_id=(grp_at(d), me_sub),
-            device_id_type=MESH,
-        )
-        copy.start()
     drain(state_send, state_sems.at[0], len(steps))
     drain(area_send, area_sems.at[0], len(steps))
-    drain(sub_parts, sub_sems.at[0], subs - 1)
 
     drain(flux_recv, flux_sems.at[1], len(steps))
     returned = flux_recv[...].reshape(routes * flux_rows, width)
@@ -332,13 +326,10 @@
             b * 16 : b * 16 + fields_atm
         ].astype(bf16)
 
-    drain(grp_parts, grp_sems.at[1], groups - 1)
-    total = grp_parts[0]
-    for i in range(1, groups):
-        total = total + grp_parts[i]
-    imbalance_out[...] = total * norm_scale
+    drain(totals, total_sems.at[1], others)
+    imbalance_out[...] = jnp.sum(totals[...], axis=0) * norm_scale
     drain(flux_send, flux_sems.at[0], len(steps))
-    drain(grp_parts, grp_sems.at[0], groups - 1)
+    drain(totals, total_sems.at[0], others)
 
 
 def finish(state_in, flux_in, total_in, state_out, flux_out, total_out, sems):
@@ -412,10 +403,8 @@
             pltpu.VMEM((ocean_blocks * 16, routes * flux_rows), bf16),
             pltpu.VMEM((routes, flux_rows, width), bf16),
             pltpu.VMEM((routes, flux_rows, width), bf16),
-            pltpu.VMEM((subs, 1, 128), f32),
-            pltpu.VMEM((groups, 1, 128), f32),
+            pltpu.VMEM((groups * subs, 1, 128), f32),
             pltpu.SemaphoreType.DMA((10,)),
-            pltpu.SemaphoreType.DMA((2,)),
             pltpu.SemaphoreType.DMA((2,)),
             pltpu.SemaphoreType.DMA((2,)),
             pltpu.SemaphoreType.DMA((2,)),

time: 23.6 us -> 22.3 us (0.945)
  Pallas kernels: 22.8 us -> 21.5 us
    pallas_call x1, Pallas kernels: 21.6 us -> 20.4 us  [shards(): pl.pallas_call(functools.partial(kernel, groups, subs, norm_scale), out_s...]
where the time goes in v6:
time: 22.3 us; the launch traced here: 22.2 us
  Pallas kernels  21.5 us (96%)
  between operations  0.64 us (3%)
    pallas_call x1, Pallas kernels, shards(): pl.pallas_call(functools.partial(kernel, groups, subs, norm_scale), out_s...  20.4 us
    pallas_call x1, Pallas kernels, shards(): pl.pallas_call(finish, out_shape=(jax.ShapeDtypeStruct(state_on_atm.shape...  1.19 us

profile of v6, /device:TPU:0, one launch (start us, length us, event | category | flops | bytes accessed | tf_op | source)
XLA Modules:
  0.0 22.2 jit_solution(16531950332392334116)
XLA Ops:
  0.6 20.4 %shard_map.121 = (bf16[8,1024]{1,0:T(8,128)(2,1)S(1)}, bf16[12,4096]{1,0:T(8,128)(2,1)S(1)}, f32[1,128]{1,0:T(1,128)S(1)}) custom-call(bf16[8,4096]{1,0:T(8,128)(2,1)} %state_hbm.1, f32[32,1,128]{2,1,0:T(1,128)} %bitcast.4, bf16[12,1024]{1,0:T(8,128)(2,1)} %flux_hbm.1, f32[8,128]{1,0:T(8,128)} %bitcast.5, f32[8,12]{1,0:T(8,128)} %bitcast.6, ...), custom_call_target="tpu_custom_call" | custom-call | tf_op jit(solution)/shard_map/pallas_call | solution.py:373
  21.0 1.2 %shard_map.122 = (bf16[8,1024]{1,0:T(8,128)(2,1)}, bf16[12,4096]{1,0:T(8,128)(2,1)}, f32[12]{0:T(128)}) custom-call(bf16[8,1024]{1,0:T(8,128)(2,1)S(1)} %get-tuple-element.6.state_in, bf16[12,4096]{1,0:T(8,128)(2,1)S(1)} %get-tuple-element.7.flux_in, f32[1,128]{1,0:T(1,128)S(1)} %get-tuple-element.8.total_in), custom_call_target="tpu_custom_call" | custom-call | tf_op jit(solution)/shard_map/pallas_call | solution.py:428

commit v7 on v6

--- a/solution.py
+++ b/solution.py
@@ -92,7 +92,9 @@
     for load in loads[:3]:
         load.start()
 
-    steps = [(o, t) for o in (0, 2) for t in range(subs)] + [(1, t) for t in range(1, subs)]
+    far = 2 * lax.rem(me_grp, 2)
+    order = (far, 2 - far, 1)
+    steps = [(o, t) for o in order[:2] for t in range(subs)] + [(1, t) for t in range(1, subs)]
 
     def grp_at(offset):
         return lax.rem(me_grp + offset + groups, groups)
@@ -149,25 +151,25 @@
             for c in range(capacity):
                 picked[(o * subs + k) * capacity + c] = block_at(o, k, c)
 
-    for o in (0, 2, 1):
+    for n, o in enumerate(order):
         for k in range(subs):
             first = (o * subs + k) * capacity
             rows = [state_wide[picked[first + c]] for c in range(capacity)]
             state_send[o * subs + k] = jnp.concatenate(rows, axis=0).astype(bf16)
-        if o == 0:
+        if n == 0:
             pl.semaphore_wait(barrier, others)
-        for t in range(1 if o == 1 else 0, subs):
+        for t in range(n // 2, subs):
             exchange(state_send, state_recv, state_sems, o, t).start()
     state_recv[subs + me_sub] = state_send[subs + me_sub]
 
     loads[3].wait()
     ocean_area_in[ocean_blocks] = jnp.zeros((1, width), f32)
-    for o in (0, 2, 1):
+    for n, o in enumerate(order):
         for k in range(subs):
             p = o * subs + k
             for c in range(capacity):
                 area_send[p, c : c + 1, :] = ocean_area_in[picked[p * capacity + c]]
-        for t in range(1 if o == 1 else 0, subs):
+        for t in range(n // 2, subs):
             exchange(area_send, area_recv, area_sems, o, t).start()
     area_recv[subs + me_sub] = area_send[subs + me_sub]
 

time: 22.3 us -> 22.4 us (level)
  no operation moved by 1% of the time
where the time goes in v7:
time: 22.4 us; the launch traced here: 22.2 us
  Pallas kernels  21.6 us (96%)
  between operations  0.64 us (3%)
    pallas_call x1, Pallas kernels, shards(): pl.pallas_call(functools.partial(kernel, groups, subs, norm_scale), out_s...  20.4 us
    pallas_call x1, Pallas kernels, shards(): pl.pallas_call(finish, out_shape=(jax.ShapeDtypeStruct(state_on_atm.shape...  1.19 us

profile of v7, /device:TPU:0, one launch (start us, length us, event | category | flops | bytes accessed | tf_op | source)
XLA Modules:
  0.0 22.2 jit_solution(14914002204780229177)
XLA Ops:
  0.6 20.4 %shard_map.121 = (bf16[8,1024]{1,0:T(8,128)(2,1)S(1)}, bf16[12,4096]{1,0:T(8,128)(2,1)S(1)}, f32[1,128]{1,0:T(1,128)S(1)}) custom-call(bf16[8,4096]{1,0:T(8,128)(2,1)} %state_hbm.1, f32[32,1,128]{2,1,0:T(1,128)} %bitcast.4, bf16[12,1024]{1,0:T(8,128)(2,1)} %flux_hbm.1, f32[8,128]{1,0:T(8,128)} %bitcast.5, f32[8,12]{1,0:T(8,128)} %bitcast.6, ...), custom_call_target="tpu_custom_call" | custom-call | tf_op jit(solution)/shard_map/pallas_call | solution.py:375
  21.0 1.2 %shard_map.122 = (bf16[8,1024]{1,0:T(8,128)(2,1)}, bf16[12,4096]{1,0:T(8,128)(2,1)}, f32[12]{0:T(128)}) custom-call(bf16[8,1024]{1,0:T(8,128)(2,1)S(1)} %get-tuple-element.6.state_in, bf16[12,4096]{1,0:T(8,128)(2,1)S(1)} %get-tuple-element.7.flux_in, f32[1,128]{1,0:T(1,128)S(1)} %get-tuple-element.8.total_in), custom_call_target="tpu_custom_call" | custom-call | tf_op jit(solution)/shard_map/pallas_call | solution.py:430
